TPU v7x, 128 devices: a whole 4x4x4 slice. The times are simulated.
128 devices in a mesh: mult: 4 (over z_lo, core), chan: 32 (over z_hi, x, y).
Axes of the slice: x: 4, y: 4, z: 4 (z_hi: 2, z_lo: 2; z = z_hi * 2 + z_lo), core: 2. Of those that a mesh axis runs over, the one named last changes fastest.
Arguments:
- columns: float32 [256, 1024, 128], P('chan'), may hold values from -6 to 6
- panels: float32 [8, 2, 1024, 1024], P('mult', None, 'chan'), may hold values from -0.1875 to 0.1875
- coefficients: float32 [256, 16, 8], P('chan', None, 'mult'), may hold values from -2 to 2
- channel_cols: int32 [256, 16], P('chan'), may hold values from 0 to 255, as said below
- used_slots: int32 [256], P('chan'), may hold values from 1 to 16, as said below
- lambda_low: int32 [256, 16], P('chan'), may hold values from 0 to 3
- lambda_high: int32 [256, 16], P('chan'), may hold values from 5 to 8
- energies: float32 [256], P('chan'), may hold values from 0 to 2
- contour: float32 [2], replicated, may hold values from 0.5 to 1.5
Outputs:
- filtered: float32 [256, 1024, 128], P('chan', 'mult')
Inputs may be any that keep to these rules, and one draw needn't show every extreme that they name: channel_cols[i, s] // 8 differs from i // 8 by at most 2, and channel_cols[i, 0] = i. `used_slots`: some channel uses all 16 slots.
All inputs are finite; a program needn't handle non-finite values.
Results may differ from a plain program's by a relative error of at most 0.0001.
Values sent between devices are 32-bit elements; how exact they have to be, the bound alone decides.
A program may use at most 192 MiB of HBM per device.

v0:
```python
import jax
import jax.numpy as jnp
from jax import lax
from jax.sharding import PartitionSpec as P

MAXNZ = 16
R = 2


def shifted(value, axis, by):
    peers = lax.axis_size(axis)
    pairs = [(i, i + by) for i in range(peers) if 0 <= i + by < peers]
    return lax.ppermute(value, axis, pairs)


def apply_panels(panels, operand, half_width):
    panel_part = lax.all_gather(panels, "chan", axis=2, tiled=True)
    real_panel = panel_part[:, 0]
    imag_panel = panel_part[:, 1]
    real_prod = jnp.einsum("lrb,cbk->clrk", real_panel, operand, precision=lax.Precision.HIGHEST)
    imag_prod = jnp.einsum("lrb,cbk->clrk", imag_panel, operand, precision=lax.Precision.HIGHEST)
    return jnp.concatenate(
        [
            real_prod[..., :half_width] - imag_prod[..., half_width:],
            real_prod[..., half_width:] + imag_prod[..., :half_width],
        ],
        axis=-1,
    )


def body(
    columns,
    panels,
    coefficients,
    channel_cols,
    used_slots,
    lambda_low,
    lambda_high,
    energies,
    contour,
):
    block_len = columns.shape[0]
    half_width = columns.shape[2] // 2
    lam_local = panels.shape[0]
    chan_index = lax.axis_index("chan")
    mult_index = lax.axis_index("mult")
    span = 2 * R + 1
    base_channel = (chan_index - R) * block_len
    local_cols = channel_cols - base_channel
    slot_ids = jnp.arange(MAXNZ, dtype=jnp.int32)
    live_slot = slot_ids[None, :] < used_slots[:, None]
    lambda_ids = mult_index * lam_local + jnp.arange(lam_local, dtype=jnp.int32)
    in_range = (lambda_ids[None, None, :] >= lambda_low[:, :, None]) & (
        lambda_ids[None, None, :] < lambda_high[:, :, None]
    )
    weights = jnp.where(
        live_slot[:, :, None] & in_range, coefficients, jnp.zeros_like(coefficients)
    )
    window_ids = jnp.arange(span * block_len, dtype=jnp.int32)
    one_hot = (local_cols[:, :, None] == window_ids[None, None, :]).astype(jnp.float32)
    mixing = jnp.einsum("isc,isl->icl", one_hot, weights, precision=lax.Precision.HIGHEST)
    shift_list = list(range(R, 0, -1)) + list(range(-1, -R - 1, -1))
    product = apply_panels(panels, columns, half_width)
    nearby = [shifted(product, "chan", distance) for distance in shift_list]
    window = jnp.concatenate(nearby[:R] + [product] + nearby[R:], axis=0)
    coupled = jnp.einsum("icl,clnk->ink", mixing, window, precision=lax.Precision.HIGHEST)
    summed = lax.psum_scatter(-coupled, "mult", scatter_dimension=1, tiled=True)
    row_count = columns.shape[1] // lax.axis_size("mult")
    own_cols = lax.dynamic_slice_in_dim(columns, mult_index * row_count, row_count, 1)
    energy_shift = (contour[0] - energies)[:, None, None]
    imag_shift = contour[1]
    real_part = own_cols[..., :half_width]
    imag_part = own_cols[..., half_width:]
    out_real = energy_shift * real_part - imag_shift * imag_part + summed[..., :half_width]
    out_imag = energy_shift * imag_part + imag_shift * real_part + summed[..., half_width:]
    return jnp.concatenate([out_real, out_imag], axis=-1)


def solution(mesh):
    return jax.shard_map(
        body,
        mesh=mesh,
        in_specs=(
            P("chan", None, None),
            P("mult", None, "chan", None),
            P("chan", None, "mult"),
            P("chan", None),
            P("chan"),
            P("chan", None),
            P("chan", None),
            P("chan"),
            P(),
        ),
        out_specs=P("chan", "mult", None),
        check_vma=False,
    )
```

profile of v0, /device:TPU:1, one launch (start us, length us, event | category | flops | bytes accessed | tf_op | source)
XLA Modules:
  0.0 1163.6 jit_solution(3106936373876137485)
XLA Ops:
  6.5 1.9 copy.11
  8.5 161.7 %all-gather.2.cloned.1.call-done = f32[2,2,1024,1024]{3,2,0,1:T(8,128)} async-done(((f32[2,2,32,1024]{3,2,0,1:T(8,128)}), f32[2,2,1024,1024]{3,2,0,1:T(8,128)}) %all-gather.2.cloned.1.call-update) | async-done | bytes 16777232 | tf_op jit(solution)/shard_map/all_gather | solution.py:17
  170.2 57.2 %fusion.4 = f32[8,2,1024,128]{2,3,1,0:T(8,128)} fusion(f32[2,2,1024,1024]{3,2,0,1:T(8,128)} %all-gather.2.cloned.1.call-done, f32[8,1024,128]{2,1,0:T(8,128)} %param.9), kind=kOutput, calls=%fused_computation.10 | convolution fusion | flops 25769803776 | bytes 20971520 | tf_op jit(solution)/shard_map/lrb,cbk->clrk/dot_general | solution.py:20
  227.4 54.3 %fusion.7 = f32[8,2,1024,128]{2,3,1,0:T(8,128)} fusion(f32[2,2,1024,1024]{3,2,0,1:T(8,128)S(1)} %copy-done.6, f32[8,1024,128]{2,1,0:T(8,128)S(1)} %copy-done.3), kind=kOutput, calls=%fused_computation.11 | convolution fusion | flops 25769803776 | bytes 20971520 | tf_op jit(solution)/shard_map/lrb,cbk->clrk/dot_general | solution.py:21
  281.7 10.3 slice_subtract_fusion
  292.1 8.3 pad_maximum_fusion
  300.4 7.9 collective-permute-start
  308.3 5.4 collective-permute-start.1
  313.8 1.3 collective-permute-start.2
  315.1 1.3 collective-permute-start.3
  316.7 167.3 %collective-permute-done = f32[8,2,1024,128]{2,3,1,0:T(8,128)} collective-permute-done((f32[8,2,1024,128]{2,3,1,0:T(8,128)}, f32[8,2,1024,128]{2,3,1,0:T(8,128)}, u32[]{:S(2)}, u32[]{:S(2)}) %collective-permute-start) | collective-permute-done | bytes 8388640 | tf_op jit(solution)/shard_map/ppermute | solution.py:13
  484.0 8.3 constant_dynamic-update-slice_fusion.4
  492.4 171.5 %collective-permute-done.1 = f32[8,2,1024,128]{2,3,1,0:T(8,128)} collective-permute-done((f32[8,2,1024,128]{2,3,1,0:T(8,128)}, f32[8,2,1024,128]{2,3,1,0:T(8,128)}, u32[]{:S(2)}, u32[]{:S(2)}) %collective-permute-start.1) | collective-permute-done | bytes 8388640 | tf_op jit(solution)/shard_map/ppermute | solution.py:13
  663.8 8.3 constant_dynamic-update-slice_fusion.3
  672.1 4.1 constant_dynamic-update-slice_fusion.2
  676.2 348.1 %collective-permute-done.2 = f32[8,2,1024,128]{2,3,1,0:T(8,128)} collective-permute-done((f32[8,2,1024,128]{2,3,1,0:T(8,128)}, f32[8,2,1024,128]{2,3,1,0:T(8,128)}, u32[]{:S(2)}, u32[]{:S(2)}) %collective-permute-start.2) | collective-permute-done | bytes 8388640 | tf_op jit(solution)/shard_map/ppermute | solution.py:13
  1024.3 8.3 constant_dynamic-update-slice_fusion.1
  1032.6 8.3 constant_dynamic-update-slice_fusion
  1040.9 43.0 %copy.14 = f32[40,2,1024,128]{3,0,1,2:T(8,128)} copy(f32[40,2,1024,128]{2,3,1,0:T(8,128)} %constant_dynamic-update-slice_fusion) | data formatting | bytes 83886080 | tf_op jit(solution)/shard_map/concatenate | solution.py:65
  1083.8 25.0 %bitcast_negate_fusion = f32[8,1024,128]{2,0,1:T(8,128)} fusion(f32[40,2,1024,128]{3,0,1,2:T(8,128)} %copy.14, f32[8,40,2]{1,2,0:T(2,128)S(1)} %fusion.10), kind=kOutput, calls=%fused_computation.9 | convolution fusion | flops 1007681536 | bytes 46139904 | tf_op jit(solution)/shard_map/icl,clnk->ink/dot_general | solution.py:66
  1109.6 2.0 constant_dynamic-slice_fusion
  1112.3 39.1 %reduce-scatter.2.cloned.1.call-done = f32[8,256,128]{2,0,1:T(8,128)} async-done(((f32[8,1024,128]{2,0,1:T(8,128)}), f32[8,256,128]{2,0,1:T(8,128)}) %reduce-scatter.2.cloned.1.call-update) | async-done | bytes 1048592 | tf_op jit(solution)/shard_map/reduce_scatter | solution.py:67
  1151.3 3.5 slice_add_fusion.2
  1155.2 1.2 copy.15
  (36 shorter events, 2.1 us)
Async XLA Ops:
  6.5 163.6 %all-gather.2.cloned.1.call-start = ((), (), s32[]{:S(2)}) async-start(), calls=%async_computation.1 | async-start | bytes 17301504 | tf_op jit(solution)/shard_map/all_gather | solution.py:17
  8.4 1142.9 %reduce-scatter.2.cloned.1.call-start = ((), (), s32[]{:S(2)}) async-start(), calls=%async_computation.2 | async-start | bytes 5242880 | tf_op jit(solution)/shard_map/reduce_scatter | solution.py:67
  170.2 57.2 %copy-start.3 = (f32[8,1024,128]{2,1,0:T(8,128)S(1)}, f32[8,1024,128]{2,1,0:T(8,128)}, u32[]{:S(2)}) copy-start(f32[8,1024,128]{2,1,0:T(8,128)} %param.9) | copy-start | bytes 12582916
  170.2 57.2 %copy-start.6 = (f32[2,2,1024,1024]{3,2,0,1:T(8,128)S(1)}, f32[2,2,1024,1024]{3,2,0,1:T(8,128)}, u32[]{:S(2)}) copy-start(f32[2,2,1024,1024]{3,2,0,1:T(8,128)} %all-gather.2.cloned.1.call-done) | copy-start | bytes 50331652
  292.0 8.4 copy-start
  292.0 24.4 %copy-start.10 = (s32[8]{0:T(128)S(1)}, s32[8]{0:T(128)}, u32[]{:S(2)}) copy-start(s32[8]{0:T(128)} %param.13) | copy-start | bytes 100
  292.0 24.4 %copy-start.4 = (s32[8,16]{1,0:T(8,128)S(1)}, s32[8,16]{1,0:T(8,128)}, u32[]{:S(2)}) copy-start(s32[8,16]{1,0:T(8,128)} %param.12) | copy-start | bytes 1540
  292.0 24.4 %copy-start.7 = (f32[8,16,2]{1,2,0:T(2,128)S(1)}, f32[8,16,2]{1,2,0:T(2,128)}, u32[]{:S(2)}) copy-start(f32[8,16,2]{1,2,0:T(2,128)} %param.11) | copy-start | bytes 3076
  292.0 24.4 %copy-start.8 = (s32[8,16]{1,0:T(8,128)S(1)}, s32[8,16]{1,0:T(8,128)}, u32[]{:S(2)}) copy-start(s32[8,16]{1,0:T(8,128)} %param.15) | copy-start | bytes 1540
  292.1 24.4 %copy-start.9 = (s32[8,16]{1,0:T(8,128)S(1)}, s32[8,16]{1,0:T(8,128)}, u32[]{:S(2)}) copy-start(s32[8,16]{1,0:T(8,128)} %param.14) | copy-start | bytes 1540
  300.4 183.6 %collective-permute-start = (f32[8,2,1024,128]{2,3,1,0:T(8,128)}, f32[8,2,1024,128]{2,3,1,0:T(8,128)}, u32[]{:S(2)}, u32[]{:S(2)}) collective-permute-start(f32[8,2,1024,128]{2,3,1,0:T(8,128)} %pad_maximum_fusion), channel_id=1, source_target_pairs={{0,2},{1,3},{2,4},{3,5},{4,6},{5,7},{6,8},{7,9},{8,10},{9,11},{10,... | collective-permute-start | bytes 25165832 | tf_op jit(solution)/shard_map/ppermute | solution.py:13
  308.3 355.5 %collective-permute-start.1 = (f32[8,2,1024,128]{2,3,1,0:T(8,128)}, f32[8,2,1024,128]{2,3,1,0:T(8,128)}, u32[]{:S(2)}, u32[]{:S(2)}) collective-permute-start(f32[8,2,1024,128]{2,3,1,0:T(8,128)} %pad_maximum_fusion), channel_id=1, source_target_pairs={{0,1},{1,2},{2,3},{3,4},{4,5},{5,6},{6,7},{7,8},{8,9},{9,10},{10,1... | collective-permute-start | bytes 25165832 | tf_op jit(solution)/shard_map/ppermute | solution.py:13
  313.8 710.5 %collective-permute-start.2 = (f32[8,2,1024,128]{2,3,1,0:T(8,128)}, f32[8,2,1024,128]{2,3,1,0:T(8,128)}, u32[]{:S(2)}, u32[]{:S(2)}) collective-permute-start(f32[8,2,1024,128]{2,3,1,0:T(8,128)} %pad_maximum_fusion), channel_id=1, source_target_pairs={{1,0},{2,1},{3,2},{4,3},{5,4},{6,5},{7,6},{8,7},{9,8},{10,9},{11,1... | collective-permute-start | bytes 25165832 | tf_op jit(solution)/shard_map/ppermute | solution.py:13
  315.1 717.5 %collective-permute-start.3 = (f32[8,2,1024,128]{2,3,1,0:T(8,128)}, f32[8,2,1024,128]{2,3,1,0:T(8,128)}, u32[]{:S(2)}, u32[]{:S(2)}) collective-permute-start(f32[8,2,1024,128]{2,3,1,0:T(8,128)} %pad_maximum_fusion), channel_id=1, source_target_pairs={{2,0},{3,1},{4,2},{5,3},{6,4},{7,5},{8,6},{9,7},{10,8},{11,9},{12,... | collective-permute-start | bytes 25165832 | tf_op jit(solution)/shard_map/ppermute | solution.py:13
  492.3 179.7 %copy-start.1 = (f32[8,2,1024,64]{2,3,1,0:T(8,128)S(1)}, f32[8,2,1024,64]{2,3,1,0:T(8,128)}, u32[]{:S(2)}) copy-start(f32[8,2,1024,64]{2,3,1,0:T(8,128)} %copy-done) | copy-start | bytes 12582916
  492.3 179.7 %copy-start.2 = (f32[8,2,1024,64]{2,3,1,0:T(8,128)S(1)}, f32[8,2,1024,64]{2,3,1,0:T(8,128)}, u32[]{:S(2)}) copy-start(f32[8,2,1024,64]{2,3,1,0:T(8,128)} %get-tuple-element.6) | copy-start | bytes 12582916
  1083.8 25.1 %copy-start.5 = (f32[2]{0:T(128)S(1)}, f32[2]{0:T(128)}, u32[]{:S(2)}) copy-start(f32[2]{0:T(128)} %param.17) | copy-start | bytes 28
  1108.9 2.8 copy-start.11
Sparse Core Ops, SparseCore 0:
  10.5 159.6 all-gather.1
  1109.0 42.2 reduce-scatter.1
where the time goes:
time: 1170 us; the launch traced here: 1160 us
  waiting for transfers between devices  888 us (76%)
  matrix products  137 us (12%)
  local copies, waits for them, and re-layouts  81.9 us (7%)
  other arithmetic  27.3 us (2%)
  starting transfers between devices  16 us (1%)
  between operations  14 us (1%)
    ppermute x4, waiting for transfers between devices, shifted(): return lax.ppermute(value, axis, pairs)  687 us
    all_gather x1, waiting for transfers between devices, apply_panels(): panel_part = lax.all_gather(panels, 'chan', axis=2, tiled=True)  162 us
    dot_general x1, matrix products, apply_panels(): jnp.einsum('lrb,cbk->clrk', real_panel, operand, precision=lax.Precision....  57.2 us
    dot_general x1, matrix products, apply_panels(): jnp.einsum('lrb,cbk->clrk', imag_panel, operand, precision=lax.Precision....  54.3 us
    concatenate x2, local copies, waits for them, and re-layouts, body(): window = jnp.concatenate(nearby[:R] + [product] + nearby[R:], axis=0)  51.3 us
    reduce_scatter x1, waiting for transfers between devices, body(): summed = lax.psum_scatter(-coupled, 'mult', scatter_dimension=1, tiled=True)  39.1 us
    unnamed x28, local copies, waits for them, and re-layouts  26.8 us
    dot_general x1, matrix products, body(): jnp.einsum('icl,clnk->ink', mixing, window, precision=lax.Precision.HIGHEST)  25 us
  transfers between devices with their start and end apart: 6, of which 5 were waited for; matrix products, arithmetic and copies ran while one was open for 3% of the time, Pallas kernels for 0%

commit v1 on v0

v1 whole, which is shorter than its diff:
```python
import jax
import jax.numpy as jnp
from jax import lax
from jax.experimental import pallas as pl
from jax.experimental.pallas import tpu as pltpu
from jax.sharding import PartitionSpec as P

MAXNZ = 16
MESH = pl.DeviceIdType.MESH
F32 = jnp.float32
BF16 = jnp.bfloat16
NB = 1024


def place():
    mi = lax.axis_index("mult")
    ci = lax.axis_index("chan")
    return mi // 2, mi % 2, ci // 16, (ci // 4) % 4, ci % 4


def device(z_lo, core, z_hi, x, y):
    return (z_lo * 2 + core, z_hi * 16 + x * 4 + y)


def split(value):
    high = value.astype(BF16)
    return high, (value - high.astype(F32)).astype(BF16)


def swap_halves(value):
    lane = lax.broadcasted_iota(jnp.int32, value.shape, value.ndim - 1)
    rolled = pltpu.roll(value, 64, value.ndim - 1)
    return jnp.where(lane < 64, -rolled, rolled)


def product_kernel(
    columns, panels, z_out,
    raw, p_high, p_low, blocks, z_buf, x_high, x_low,
    own_sem, first_send, p_send, p_recv, x_send, x_recv, s_send, s_recv, z_sem,
):
    z_lo, core, z_hi, x, y = place()
    left_x, right_x = (x + 3) % 4, (x + 1) % 4
    left_y, right_y = (y + 3) % 4, (y + 1) % 4
    to_left_x = device(z_lo, core, z_hi, left_x, y)
    to_right_x = device(z_lo, core, z_hi, right_x, y)
    to_left_y = device(z_lo, core, z_hi, x, left_y)
    to_right_y = device(z_lo, core, z_hi, x, right_y)
    sibling = device(z_lo, 1 - core, z_hi, x, y)
    target_x = (x + 2 * core + 3) % 4
    targets = [device(z_hi, x // 2, zh, target_x, y) for zh in range(2)]

    def origin(at_x):
        row_part = 1 - at_x % 2
        from_x = 2 * core + row_part
        from_core = jnp.where((from_x + 1) % 4 == at_x, 1, 0)
        return row_part, from_x, from_core

    row_part0, from_x0, from_core0 = origin(x)
    sources = [device(zl, from_core0, z_lo, from_x0, y) for zl in range(2)]
    spots = [origin(at) for at in (x, left_x, right_x, (x + 2) % 4)]

    barrier = pltpu.get_barrier_semaphore()
    peers = [to_left_x, to_right_x, to_left_y, to_right_y, sibling] + targets + sources
    for peer in peers:
        pl.semaphore_signal(barrier, inc=1, device_id=peer, device_id_type=MESH)
    pl.semaphore_wait(barrier, len(peers))

    def remote(src, dst, send_sem, recv_sem, peer):
        return pltpu.make_async_remote_copy(
            src_ref=src, dst_ref=dst, send_sem=send_sem, recv_sem=recv_sem,
            device_id=peer, device_id_type=MESH,
        )

    def piece(q):
        return pl.ds(4 * core + 2 * q, 2)

    def other_piece(q):
        return pl.ds(4 * (1 - core) + 2 * q, 2)

    sent = []

    def start(copy):
        copy.start()
        sent.append(copy)

    for k in range(2):
        start(remote(panels, raw.at[0, z_lo], first_send.at[k], p_recv.at[0, z_lo], targets[k]))
    for k, (q_right, q_left) in enumerate(((0, 1), (1, 0))):
        start(remote(columns.at[piece(q_right)], blocks.at[1, piece(q_right)],
                     x_send.at[0, q_right], x_recv.at[1, q_right], to_right_y))
        start(remote(columns.at[piece(q_left)], blocks.at[2, piece(q_left)],
                     x_send.at[1, q_left], x_recv.at[2, q_left], to_left_y))
    own = pltpu.make_async_copy(columns, blocks.at[0], own_sem)
    own.start()

    def wait_p(slot, zl):
        remote(raw.at[slot, zl], raw.at[slot, zl], p_send.at[0, zl], p_recv.at[slot, zl], to_right_x).wait_recv()

    def wait_x(block, q):
        ref = blocks.at[block, piece(q)]
        remote(ref, ref, x_send.at[0, q], x_recv.at[block, q], to_right_y).wait_recv()

    def to_sibling(block, q):
        ref = blocks.at[block, piece(q)]
        start(remote(ref, ref, s_send.at[block, q], s_recv.at[block, q], sibling))

    def wait_sibling(block, q):
        ref = blocks.at[block, other_piece(q)]
        remote(ref, ref, s_send.at[block, q], s_recv.at[block, q], sibling).wait_recv()

    def convert(slot):
        row_part, _, from_core = spots[slot]
        for zl in range(2):
            for order in range(2):
                at = row_part * 8 + 4 * zl + 2 * from_core + order
                for ri in range(2):
                    high, low = split(raw[slot, zl, order, ri])
                    p_high[at, ri] = high
                    p_low[at, ri] = low

    def load_piece(block, first):
        both = jnp.concatenate([blocks[block, first], blocks[block, first + 1]], axis=1)
        high, low = split(both)
        x_high[...] = high
        x_low[...] = low

    def multiply(ph, plo):
        high = x_high[...]
        acc = jnp.dot(ph, high, preferred_element_type=F32)
        acc += jnp.dot(plo, high, preferred_element_type=F32)
        acc += jnp.dot(ph, x_low[...], preferred_element_type=F32)
        return acc

    def store(acc, count, at, channel):
        acc = acc.reshape(count, 2, 32, 256)
        for half in range(2):
            part = acc[..., half * 128:half * 128 + 128]
            z_buf[channel + half, pl.ds(at, count)] = part[:, 0] + swap_halves(part[:, 1])

    def own_times(slot):
        row_part, _, from_core = spots[slot]

        def body(k, carry):
            load_piece(0, 2 * k)
            ats = [row_part * 8 + 4 * zl + 2 * from_core for zl in range(2)]
            ph = jnp.concatenate([p_high[pl.ds(at, 2)] for at in ats], axis=0).reshape(256, NB)
            plo = jnp.concatenate([p_low[pl.ds(at, 2)] for at in ats], axis=0).reshape(256, NB)
            acc = multiply(ph, plo)
            for zl in range(2):
                store(acc[zl * 128:zl * 128 + 128], 2, ats[zl], y * 8 + 2 * k)
            return carry

        lax.fori_loop(0, 4, body, 0)

    def piece_times(block, at_y, firsts):
        def body(k, carry):
            first = firsts(k)
            load_piece(block, first)

            def rows(part, inner):
                ph = p_high[pl.ds(part * 8, 8)].reshape(512, NB)
                plo = p_low[pl.ds(part * 8, 8)].reshape(512, NB)
                store(multiply(ph, plo), 8, part * 8, at_y * 8 + first)
                return inner

            lax.fori_loop(0, 2, rows, 0)
            return carry

        lax.fori_loop(0, 2, body, 0)

    def z_copy(block, at_y):
        part = pl.ds(at_y * 8, 8)
        return pltpu.make_async_copy(z_buf.at[part], z_out.at[part], z_sem.at[block])

    for zl in range(2):
        wait_p(0, zl)
    for zl_right, zl_left in ((0, 1), (1, 0)):
        start(remote(raw.at[0, zl_right], raw.at[1, zl_right], p_send.at[0, zl_right],
                     p_recv.at[1, zl_right], to_right_x))
        start(remote(raw.at[0, zl_left], raw.at[2, zl_left], p_send.at[1, zl_left],
                     p_recv.at[2, zl_left], to_left_x))
    convert(0)
    own.wait()
    own_times(0)

    wait_x(1, 0)
    start(remote(blocks.at[1, piece(0)], blocks.at[3, piece(0)], x_send.at[2, 0], x_recv.at[3, 0], to_right_y))
    to_sibling(1, 0)
    wait_x(2, 1)
    start(remote(blocks.at[2, piece(1)], blocks.at[3, piece(1)], x_send.at[2, 1], x_recv.at[3, 1], to_left_y))
    to_sibling(2, 1)

    wait_p(1, 0)
    start(remote(raw.at[1, 0], raw.at[3, 0], p_send.at[2, 0], p_recv.at[3, 0], to_right_x))
    wait_p(2, 1)
    start(remote(raw.at[2, 1], raw.at[3, 1], p_send.at[2, 1], p_recv.at[3, 1], to_left_x))
    wait_p(1, 1)
    convert(1)
    own_times(1)
    wait_p(2, 0)
    convert(2)
    own_times(2)
    wait_x(1, 1)
    to_sibling(1, 1)
    wait_x(2, 0)
    to_sibling(2, 0)
    wait_p(3, 0)
    wait_p(3, 1)
    convert(3)
    own_times(3)
    out_copies = [z_copy(0, y)]
    out_copies[-1].start()

    for block, at_y in ((1, left_y), (2, right_y), (3, (y + 2) % 4)):
        if block == 3:
            for q in range(2):
                wait_x(3, q)
                to_sibling(3, q)
        piece_times(block, at_y, lambda k: 4 * core + 2 * k)
        for q in range(2):
            wait_sibling(block, q)
        piece_times(block, at_y, lambda k: 4 * (1 - core) + 2 * k)
        out_copies.append(z_copy(block, at_y))
        out_copies[-1].start()

    for copy in sent:
        copy.wait_send()
    for copy in out_copies:
        copy.wait()


def product(columns, panels):
    dma = pltpu.SemaphoreType.DMA
    return pl.pallas_call(
        product_kernel,
        out_shape=jax.ShapeDtypeStruct((32, 16, 32, 128), F32),
        in_specs=[pl.BlockSpec(memory_space=pl.ANY)] * 2,
        out_specs=pl.BlockSpec(memory_space=pl.ANY),
        scratch_shapes=[
            pltpu.VMEM((4, 2, 2, 2, 32, NB), F32),
            pltpu.VMEM((16, 2, 32, NB), BF16),
            pltpu.VMEM((16, 2, 32, NB), BF16),
            pltpu.VMEM((4, 8, NB, 128), F32),
            pltpu.VMEM((32, 16, 32, 128), F32),
            pltpu.VMEM((NB, 256), BF16),
            pltpu.VMEM((NB, 256), BF16),
            dma, dma((2,)), dma((3, 2)), dma((4, 2)), dma((3, 2)), dma((4, 2)), dma((4, 2)), dma((4, 2)), dma((4,)),
        ],
        compiler_params=pltpu.CompilerParams(
            collective_id=0, has_side_effects=True, vmem_limit_bytes=52 * 2**20
        ),
        cost_estimate=pl.CostEstimate(flops=26_000_000_000, bytes_accessed=40_000_000, transcendentals=0),
        name="product",
    )(columns, panels)


def mix_kernel(
    z_in, mix, columns, shift, turn, out,
    z_buf, mix_high, mix_low, coupled, near, far, own_cols,
    z_sem, col_sem, send_sem, near_sem, far_sem,
):
    mi = lax.axis_index("mult")
    ci = lax.axis_index("chan")
    group, y = ci // 4, ci % 4
    below, above = (group + 7) % 8, (group + 1) % 8
    target = [(mi, below * 4 + 2), (mi, below * 4 + 3)]
    target += [(mi, group * 4 + k) for k in range(4)]
    target += [(mi, above * 4), (mi, above * 4 + 1)]
    outer = jnp.where(y < 2, below, above)

    loads = []
    for t in range(4):
        part = pl.ds(t * 8, 8)
        loads.append(pltpu.make_async_copy(z_in.at[part], z_buf.at[part], z_sem.at[t]))
        loads[-1].start()
    col_load = pltpu.make_async_copy(columns.at[:, pl.ds(mi * 256, 256)], own_cols, col_sem)
    col_load.start()

    barrier = pltpu.get_barrier_semaphore()
    for w in (0, 1, 6, 7):
        pl.semaphore_signal(barrier, inc=1, device_id=target[w], device_id_type=MESH)
    for k in range(4):
        pl.semaphore_signal(barrier, inc=1, device_id=(mi, outer * 4 + k), device_id_type=MESH)
    for k in range(1, 4):
        pl.semaphore_signal(barrier, inc=1, device_id=(mi, group * 4 + (y + k) % 4), device_id_type=MESH)
    pl.semaphore_wait(barrier, 11)

    lane = lax.broadcasted_iota(jnp.int32, (320, 512), 1)
    row = lax.broadcasted_iota(jnp.int32, (320, 512), 0)
    same = (lane % 8) == (row % 8)
    for t in range(4):
        wide = jnp.broadcast_to(mix[t][:, None, :], (40, 8, 512)).reshape(320, 512)
        high, low = split(jnp.where(same, wide, 0.0))
        mix_high[t] = high
        mix_low[t] = low

    def far_copy(w):
        return pltpu.make_async_remote_copy(
            src_ref=coupled.at[w], dst_ref=far.at[y], send_sem=send_sem.at[w], recv_sem=far_sem.at[y],
            device_id=target[w], device_id_type=MESH,
        )

    def near_copy(w):
        return pltpu.make_async_remote_copy(
            src_ref=coupled.at[w], dst_ref=near.at[y], send_sem=send_sem.at[w], recv_sem=near_sem.at[y],
            device_id=target[w], device_id_type=MESH,
        )

    def send_near(w):
        @pl.when(y != w - 2)
        def _():
            near_copy(w).start()

        @pl.when(y == w - 2)
        def _():
            pltpu.make_async_copy(coupled.at[w], near.at[y], near_sem.at[y]).start()

    for t in range(4):
        loads[t].wait()

        def body(k, carry):
            part, first = k // 2, pl.multiple_of((k % 2) * 16, 16)
            tile = z_buf[pl.ds(t * 8, 8), pl.ds(part * 8, 8), pl.ds(first, 16), :]
            both = jnp.concatenate(
                [tile[:, :, :8].reshape(512, 128), tile[:, :, 8:].reshape(512, 128)], axis=1
            )
            high, low = split(both)
            acc = jnp.dot(mix_high[t], high, preferred_element_type=F32)
            acc += jnp.dot(mix_high[t], low, preferred_element_type=F32)
            acc += jnp.dot(mix_low[t], high, preferred_element_type=F32)
            for half in range(2):
                new = acc[:, half * 128:half * 128 + 128].reshape(5, 8, 8, 128)
                at = pl.multiple_of(first + half * 8, 8)
                if t > 0:
                    coupled[pl.ds(t, 4), :, part, pl.ds(at, 8), :] += new[:4]
                    coupled[t + 4, :, part, pl.ds(at, 8), :] = new[4]
                else:
                    coupled[pl.ds(0, 5), :, part, pl.ds(at, 8), :] = new
            return carry

        lax.fori_loop(0, 4, body, 0)
        if t < 2:
            far_copy(t).start()
        if t == 2:
            send_near(2)
    far_copy(6).start()
    far_copy(7).start()
    for w in (3, 4, 5):
        send_near(w)

    col_load.wait()
    for k in range(4):
        pltpu.make_async_copy(coupled.at[0], near.at[k], near_sem.at[k]).wait()
        pltpu.make_async_copy(coupled.at[0], far.at[k], far_sem.at[k]).wait()
        for part in range(2):
            rows = pl.ds(part * 128 + k * 32, 32)
            cols = own_cols[:, rows, :]
            out[:, rows, :] = (
                shift[...] * cols + turn[...] * pltpu.roll(cols, 64, 2) - (near[k, :, part] + far[k, :, part])
            )

    for w in (0, 1, 6, 7):
        far_copy(w).wait_send()
    for w in (2, 3, 4, 5):
        @pl.when(y != w - 2)
        def _():
            near_copy(w).wait_send()


def mix_and_finish(z, mix, columns, shift, turn):
    dma = pltpu.SemaphoreType.DMA
    vmem = pl.BlockSpec(memory_space=pltpu.VMEM)
    anywhere = pl.BlockSpec(memory_space=pl.ANY)
    return pl.pallas_call(
        mix_kernel,
        out_shape=jax.ShapeDtypeStruct((8, 256, 128), F32),
        in_specs=[anywhere, vmem, anywhere, vmem, vmem],
        out_specs=vmem,
        scratch_shapes=[
            pltpu.VMEM((32, 16, 32, 128), F32),
            pltpu.VMEM((4, 320, 512), BF16),
            pltpu.VMEM((4, 320, 512), BF16),
            pltpu.VMEM((8, 8, 2, 32, 128), F32),
            pltpu.VMEM((4, 8, 2, 32, 128), F32),
            pltpu.VMEM((4, 8, 2, 32, 128), F32),
            pltpu.VMEM((8, 256, 128), F32),
            dma((4,)), dma, dma((8,)), dma((4,)), dma((4,)),
        ],
        compiler_params=pltpu.CompilerParams(
            collective_id=1, has_side_effects=True, vmem_limit_bytes=40 * 2**20
        ),
        cost_estimate=pl.CostEstimate(flops=4_000_000_000, bytes_accessed=12_000_000, transcendentals=0),
        name="mix",
    )(z, mix, columns, shift, turn)


def mixing_rows(coefficients, channel_cols, used_slots, lambda_low, lambda_high):
    mi = lax.axis_index("mult")
    ci = lax.axis_index("chan")
    slot_ids = jnp.arange(MAXNZ, dtype=jnp.int32)
    live_slot = slot_ids[None, :] < used_slots[:, None]
    lambda_ids = mi * 2 + jnp.arange(2, dtype=jnp.int32)
    in_range = (lambda_ids >= lambda_low[:, :, None]) & (lambda_ids < lambda_high[:, :, None])
    weights = jnp.where(live_slot[:, :, None] & in_range, coefficients, jnp.zeros_like(coefficients))
    packed = jnp.concatenate([weights, channel_cols[:, :, None].astype(F32)], axis=2)
    whole = lax.all_gather(packed, ("mult", "chan"), axis=0, tiled=False).reshape(4, 32, 8, MAXNZ, 3)
    ring = jnp.concatenate([whole[:, -2:], whole, whole[:, :2]], axis=1)
    group = ci // 4
    near = lax.dynamic_slice_in_dim(ring, group * 4, 8, 1)
    weight = jnp.transpose(near[..., :2], (1, 2, 3, 0, 4)).reshape(64, MAXNZ, 8)
    cols = near[0, :, :, :, 2].reshape(64, MAXNZ) - (group * 32).astype(F32)
    hit = cols[:, :, None] == jnp.arange(32, dtype=jnp.int32).astype(F32)
    mixing = jnp.sum(jnp.where(hit[:, :, :, None], weight[:, :, None, :], 0.0), axis=1)
    parts = [mixing[8 * t:8 * t + 40, 8 * t:8 * t + 8].reshape(40, 64) for t in range(4)]
    return jnp.repeat(jnp.stack(parts), 8, axis=2)


def body(
    columns, panels, coefficients, channel_cols, used_slots, lambda_low, lambda_high, energies, contour
):
    mix = mixing_rows(coefficients, channel_cols, used_slots, lambda_low, lambda_high)
    z = product(columns, panels)
    shift = jnp.broadcast_to((contour[0] - energies)[:, None, None], (8, 1, 128))
    lane = jnp.arange(128, dtype=jnp.int32)
    turn = jnp.where(lane < 64, -contour[1], contour[1])[None, None, :]
    return mix_and_finish(z, mix, columns, shift, turn)


def solution(mesh):
    return jax.shard_map(
        body,
        mesh=mesh,
        in_specs=(
            P("chan", None, None),
            P("mult", None, "chan", None),
            P("chan", None, "mult"),
            P("chan", None),
            P("chan"),
            P("chan", None),
            P("chan", None),
            P("chan"),
            P(),
        ),
        out_specs=P("chan", "mult", None),
        check_vma=False,
    )
```

time: 1170 us -> 510 us (0.44)
  waiting for transfers between devices: 888 us -> 0 us
  blocking collectives: 0 us -> 340 us
  Pallas kernels: 0 us -> 152 us
  matrix products: 137 us -> 0 us
  local copies, waits for them, and re-layouts: 81.9 us -> 6.97 us
  other arithmetic: 27.3 us -> 4.76 us
  starting transfers between devices: 16 us -> 0 us
  between operations: 14 us -> 0.78 us
    ppermute x4 -> x0, waiting for transfers between devices: 687 us -> none  [shifted(): return lax.ppermute(value, axis, pairs)]
    all_gather x0 -> x1, blocking collectives: none -> 340 us  [mixing_rows(): lax.all_gather(packed, ('mult', 'chan'), axis=0, tiled=False)]
    all_gather x1 -> x0, waiting for transfers between devices: 162 us -> none  [apply_panels(): panel_part = lax.all_gather(panels, 'chan', axis=2, tiled=True)]
    pallas_call x0 -> x2, Pallas kernels: none -> 152 us  [the longest x1 105 us: product(): pl.pallas_call(product_kernel, out_shape=jax.ShapeDtypeStruct((32, 16, 32...]
    dot_general x4 -> x0, matrix products: 137 us -> none  [the longest x1 57.2 us: apply_panels(): jnp.einsum('lrb,cbk->clrk', real_panel, operand, precision=lax.Precision....]
    concatenate x3 -> x0, local copies, waits for them, and re-layouts: 52.4 us -> none  [the longest x2 51.3 us: body(): window = jnp.concatenate(nearby[:R] + [product] + nearby[R:], axis=0)]
    reduce_scatter x1 -> x0, waiting for transfers between devices: 39.1 us -> none  [body(): summed = lax.psum_scatter(-coupled, 'mult', scatter_dimension=1, tiled=True)]
    unnamed x28 -> x7, local copies, waits for them, and re-layouts: 26.8 us -> 4.89 us
  transfers between devices with their start and end apart: 6 -> 0, of which waited for: 5 -> 0; matrix products, arithmetic and copies ran while one was open for 3% -> 0% of each run, Pallas kernels for 0% -> 0%
where the time goes in v1:
time: 510 us; the launch traced here: 505 us
  blocking collectives  340 us (67%)
  Pallas kernels  152 us (30%)
  local copies, waits for them, and re-layouts  6.97 us (1%)
    all_gather x1, blocking collectives, mixing_rows(): lax.all_gather(packed, ('mult', 'chan'), axis=0, tiled=False)  340 us
    pallas_call x1, Pallas kernels, product(): pl.pallas_call(product_kernel, out_shape=jax.ShapeDtypeStruct((32, 16, 32...  105 us
    pallas_call x1, Pallas kernels, mix_and_finish(): pl.pallas_call(mix_kernel, out_shape=jax.ShapeDtypeStruct((8, 256, 128),...  47.7 us

profile of v1, /device:TPU:1, one launch (start us, length us, event | category | flops | bytes accessed | tf_op | source)
XLA Modules:
  0.0 504.6 jit_solution(11535011291546877761)
XLA Ops:
  0.0 0.7 iota_compare_fusion
  0.7 1.3 fusion.4
  2.7 0.7 compare_select_fusion.turn
  3.4 1.3 broadcast_subtract_fusion
  4.6 0.1 broadcast_in_dim.60.shift
  4.7 0.7 convert_bitcast_fusion
  5.4 0.8 copy_select_fusion
  6.2 339.6 %all-gather = f32[1024,16,3]{1,0,2:T(8,128)S(1)} all-gather(f32[8,16,3]{1,0,2:T(8,128)S(1)} %pad_maximum_fusion.1), channel_id=2, replica_groups=mesh['mult'=4,'chan'=32] {'mult','chan'}, dimensions={0}, use_global_device_ids=true | all-gather | bytes 198144 | tf_op jit(solution)/shard_map/all_gather | solution.py:406
  345.9 0.1 fusion.1
  346.0 0.1 copy.59
  346.1 0.1 copy.61
  346.2 0.1 broadcast_compare_fusion
  346.3 0.4 select_reduce_fusion
  346.7 0.0 copy-start.1
  346.7 0.1 slice_bitcast_fusion.4
  346.8 0.1 broadcast_bitcast_fusion
  346.9 0.3 copy.62.mix
  347.2 0.5 copy-done.1
  347.8 104.7 %product.1.z_in = f32[32,16,32,128]{3,2,1,0:T(8,128)} custom-call(f32[8,1024,128]{2,1,0:T(8,128)} %columns.3, f32[2,2,32,1024]{3,2,1,0:T(8,128)S(1)} %copy-done.1), custom_call_target="tpu_custom_call" | custom-call | flops 25999998976 | bytes 40000000 | tf_op jit(solution)/shard_map/product/pallas_call | solution.py:234
  452.5 0.0 copy-done
  452.5 0.0 copy-start.2
  452.5 3.4 copy-done.2
  455.9 47.7 %mix.1 = f32[8,256,128]{2,1,0:T(8,128)S(1)} custom-call(f32[32,16,32,128]{3,2,1,0:T(8,128)S(1)} %copy-done.2, f32[4,40,512]{2,1,0:T(8,128)S(1)} %copy.62.mix, f32[8,1024,128]{2,1,0:T(8,128)S(1)} %copy-done, f32[8,1,128]{2,1,0:T(1,128)S(1)} %broadcast_in_dim.60.shift, f32[1,1,128]{2,1,0:T(1,128)S(1)} %compare_select_fusion.turn), custom_call_target="tpu_custom_call" | custom-call | flops 4000000000 | bytes 12000000 | tf_op jit(solution)/shard_map/mix/pallas_call | solution.py:374
  503.6 1.0 copy.69
  (9 shorter events, 0.1 us)
Async XLA Ops:
  346.7 1.0 copy-start.1
  347.8 104.7 %copy-start = (f32[8,1024,128]{2,1,0:T(8,128)S(1)}, f32[8,1024,128]{2,1,0:T(8,128)}, u32[]{:S(2)}) copy-start(f32[8,1024,128]{2,1,0:T(8,128)} %columns.3) | copy-start | bytes 12582916
  452.5 3.4 copy-start.2

commit v2 on v0

v2 whole, which is shorter than its diff:
```python
import jax
import jax.numpy as jnp
from jax import lax
from jax.experimental import pallas as pl
from jax.experimental.pallas import tpu as pltpu
from jax.sharding import PartitionSpec as P

MAXNZ = 16
MESH = pl.DeviceIdType.MESH
F32 = jnp.float32
BF16 = jnp.bfloat16
NB = 1024


def device(z_lo, core, z_hi, x, y):
    return (z_lo * 2 + core, z_hi * 16 + x * 4 + y)


def split(value):
    high = value.astype(BF16)
    return high, (value - high.astype(F32)).astype(BF16)


def swap_halves(value):
    lane = lax.broadcasted_iota(jnp.int32, value.shape, value.ndim - 1)
    rolled = pltpu.roll(value, 64, value.ndim - 1)
    return jnp.where(lane < 64, -rolled, rolled)


def kernel(
    columns, panels, mine, shift, turn, out,
    raw, p_high, p_low, blocks, x_high, x_low, z_first, z_second,
    parts, mix_full, mix_rows, mix_high, mix_low, coupled, near, far,
    own_sem, first_send, p_send, p_recv, x_send, f_send, z_send, x_recv, s_send, s_recv,
    part_send, part_recv, row_send, row_recv, c_send, near_sem, far_sem,
):
    mi = lax.axis_index("mult")
    ci = lax.axis_index("chan")
    z_lo, core, z_hi, x, y = mi // 2, mi % 2, ci // 16, (ci // 4) % 4, ci % 4
    left_x, right_x = (x + 3) % 4, (x + 1) % 4
    left_y, right_y = (y + 3) % 4, (y + 1) % 4
    to_left_x = device(z_lo, core, z_hi, left_x, y)
    to_right_x = device(z_lo, core, z_hi, right_x, y)
    to_left_y = device(z_lo, core, z_hi, x, left_y)
    to_right_y = device(z_lo, core, z_hi, x, right_y)
    sibling = device(z_lo, 1 - core, z_hi, x, y)
    partner = device(1 - z_lo, core, z_hi, x, y)
    full = z_lo == core
    target_x = (x + 2 * core + 3) % 4
    targets = [device(z_hi, x // 2, zh, target_x, y) for zh in range(2)]

    def origin(at_x):
        row_part = 1 - at_x % 2
        from_x = 2 * core + row_part
        from_core = jnp.where((from_x + 1) % 4 == at_x, 1, 0)
        return row_part, from_x, from_core

    _, from_x0, from_core0 = origin(x)
    sources = [device(zl, from_core0, z_lo, from_x0, y) for zl in range(2)]
    spots = [origin(at) for at in (x, left_x, right_x, (x + 2) % 4)]
    first_part, second_part = x % 2, 1 - x % 2

    group = ci // 4
    below, above = (group + 7) % 8, (group + 1) % 8
    owners = [(mi, below * 4 + 2), (mi, below * 4 + 3)]
    owners += [(mi, group * 4 + k) for k in range(4)]
    owners += [(mi, above * 4), (mi, above * 4 + 1)]
    outer = jnp.where(y < 2, below, above)
    outer_spot = jnp.where(y < 2, y + 6, y - 2)
    helpers = [(mi, outer * 4 + k) for k in range(4)]
    mates = [(mi, group * 4 + (y + k) % 4) for k in range(1, 4)]
    others = [((mi + k) % 4, ci) for k in range(1, 4)]

    barrier = pltpu.get_barrier_semaphore()
    peers = [to_left_x, to_right_x] + targets + sources + others + mates + helpers
    peers += [owners[w] for w in (0, 1, 6, 7)]
    for peer in peers:
        pl.semaphore_signal(barrier, inc=1, device_id=peer, device_id_type=MESH)
    pl.semaphore_wait(barrier, len(peers))

    def remote(src, dst, send_sem, recv_sem, peer):
        return pltpu.make_async_remote_copy(
            src_ref=src, dst_ref=dst, send_sem=send_sem, recv_sem=recv_sem,
            device_id=peer, device_id_type=MESH,
        )

    sent = []
    sent_full = []

    def start(copy):
        copy.start()
        sent.append(copy)

    for k in range(2):
        start(remote(panels, raw.at[0, z_lo], first_send.at[k], p_recv.at[0, z_lo], targets[k]))

    def channel(e, s):
        return 4 * core + 2 * e + s

    def own_copies(e):
        copies = []
        for s_right, s_left in ((0, 1), (1, 0)):
            c_right, c_left = channel(e, s_right), channel(e, s_left)
            copies.append(remote(columns.at[c_right], blocks.at[1, c_right],
                                 x_send.at[0, e, s_right], x_recv.at[1, e, s_right], to_right_y))
            copies.append(remote(columns.at[c_left], blocks.at[2, c_left],
                                 x_send.at[1, e, s_left], x_recv.at[2, e, s_left], to_left_y))
        return copies

    common, extra = own_copies(0), own_copies(1)
    for copy in common[:2]:
        start(copy)

    @pl.when(full)
    def _():
        for copy in extra[:2]:
            copy.start()

    for copy in common[2:]:
        start(copy)

    @pl.when(full)
    def _():
        for copy in extra[2:]:
            copy.start()

    sent_full += extra

    own = pltpu.make_async_copy(columns, blocks.at[0], own_sem)
    own.start()
    for k in range(3):
        start(remote(mine, parts.at[2 - k], part_send.at[k], part_recv.at[2 - k], others[k]))

    def wait_p(slot, zl):
        ref = raw.at[slot, zl]
        remote(ref, ref, p_send.at[0, zl], p_recv.at[slot, zl], to_right_x).wait_recv()

    def forward_p(zl):
        slot, peer = (1, to_right_x) if zl == 0 else (2, to_left_x)
        start(remote(raw.at[slot, zl], raw.at[3, zl], p_send.at[2, zl], p_recv.at[3, zl], peer))

    def wait_x(b, e, s):
        ref = blocks.at[b, channel(e, s)]
        remote(ref, ref, x_send.at[0, e, s], x_recv.at[b, e, s], to_right_y).wait_recv()

    def forward_x(e, s):
        c = channel(e, s)
        b, peer = (1, to_right_y) if s == 0 else (2, to_left_y)
        return remote(blocks.at[b, c], blocks.at[3, c], f_send.at[e, s], x_recv.at[3, e, s], peer)

    def to_partner(b, s):
        ref = blocks.at[b, channel(1, s)]
        return remote(ref, ref, z_send.at[b, s], x_recv.at[b, 1, s], partner)

    def to_sibling(b, e, s):
        ref = blocks.at[b, channel(e, s)]
        start(remote(ref, ref, s_send.at[b, e, s], s_recv.at[b, e, s], sibling))

    def wait_sibling(b):
        for e in range(2):
            for s in range(2):
                ref = blocks.at[b, 4 * (1 - core) + 2 * e + s]
                remote(ref, ref, s_send.at[b, e, s], s_recv.at[b, e, s], sibling).wait_recv()

    def take_extra(pairs, onward):
        @pl.when(full)
        def _():
            for b, s in pairs:
                wait_x(b, 1, s)
                if onward:
                    forward_x(1, s).start()
                to_partner(b, s).start()

        for b, s in pairs:
            if onward:
                sent_full.append(forward_x(1, s))
            sent_full.append(to_partner(b, s))

    def pass_extra(pairs):
        @pl.when(jnp.logical_not(full))
        def _():
            for b, s in pairs:
                wait_x(b, 1, s)

        for b, s in pairs:
            to_sibling(b, 1, s)

    def convert_p(slot):
        row_part, _, from_core = spots[slot]
        for zl in range(2):
            for order in range(2):
                at = row_part * 8 + 4 * zl + 2 * from_core + order
                for ri in range(2):
                    high, low = split(raw[slot, zl, order, ri])
                    p_high[at, ri] = high
                    p_low[at, ri] = low

    def convert_x(b, first, count):
        def step(k, carry):
            piece = first + k
            both = jnp.concatenate([blocks[b, 2 * piece], blocks[b, 2 * piece + 1]], axis=1)
            high, low = split(both)
            x_high[b * 4 + piece] = high
            x_low[b * 4 + piece] = low
            return carry

        lax.fori_loop(0, count, step, 0)

    def multiply(ph, plo, piece):
        acc = jnp.dot(ph, x_high[piece], preferred_element_type=F32)
        acc += jnp.dot(plo, x_high[piece], preferred_element_type=F32)
        acc += jnp.dot(ph, x_low[piece], preferred_element_type=F32)
        return acc

    def store(ref, acc, count, at, chan):
        acc = acc.reshape(count, 2, 32, 256)
        for half in range(2):
            part = acc[..., half * 128:half * 128 + 128]
            ref[chan + half, pl.ds(at, count)] = part[:, 0] + swap_halves(part[:, 1])

    def unit_slot(slot, b):
        row_part, _, from_core = spots[slot]
        ats = [4 * zl + 2 * from_core for zl in range(2)]

        def step(k, carry):
            ph = jnp.concatenate([p_high[pl.ds(row_part * 8 + at, 2)] for at in ats], axis=0)
            plo = jnp.concatenate([p_low[pl.ds(row_part * 8 + at, 2)] for at in ats], axis=0)
            acc = multiply(ph.reshape(256, NB), plo.reshape(256, NB), b * 4 + k)
            for zl in range(2):
                store(z_second, acc[zl * 128:zl * 128 + 128], 2, ats[zl], b * 8 + 2 * k)
            return carry

        lax.fori_loop(0, 4, step, 0)

    def unit_first(b):
        def step(k, carry):
            ph = p_high[pl.ds(first_part * 8, 8)].reshape(512, NB)
            plo = p_low[pl.ds(first_part * 8, 8)].reshape(512, NB)
            store(z_first, multiply(ph, plo, b * 4 + k), 8, 0, 2 * k)
            return carry

        lax.fori_loop(0, 4, step, 0)

    at_y = [y, left_y, right_y, (y + 2) % 4]

    def mix(ref, base, b, part):
        t = at_y[b]

        def step(k, carry):
            first = pl.multiple_of(k * 16, 16)
            tile = ref[pl.ds(base, 8), :, pl.ds(first, 16), :]
            both = jnp.concatenate(
                [tile[:, :, :8].reshape(512, 128), tile[:, :, 8:].reshape(512, 128)], axis=1
            )
            high, low = split(both)
            acc = jnp.dot(mix_high[t], high, preferred_element_type=F32)
            acc += jnp.dot(mix_high[t], low, preferred_element_type=F32)
            acc += jnp.dot(mix_low[t], high, preferred_element_type=F32)
            for half in range(2):
                new = acc[:, half * 128:half * 128 + 128].reshape(5, 8, 8, 128)
                at = pl.multiple_of(first + half * 8, 8)
                coupled[part, pl.ds(t, 5), :, pl.ds(at, 8), :] += new
            return carry

        lax.fori_loop(0, 2, step, 0)

    def far_copy(part, w):
        return remote(coupled.at[part, w], far.at[part, y], c_send.at[part, w], far_sem.at[part, y], owners[w])

    def near_copy(part, w):
        return remote(coupled.at[part, w], near.at[part, y], c_send.at[part, w], near_sem.at[part, y], owners[w])

    def send_coupled(part):
        for w in (0, 1, 6, 7):
            far_copy(part, w).start()
        for w in (2, 3, 4, 5):
            @pl.when(y != w - 2)
            def _():
                near_copy(part, w).start()

        pltpu.make_async_copy(coupled.at[part, y + 2], near.at[part, y], near_sem.at[part, y]).start()

    def build_mix():
        wide_row = lax.broadcasted_iota(jnp.int32, (128, 512), 0)
        wide_lane = lax.broadcasted_iota(jnp.int32, (128, 512), 1)
        widen = jnp.where(wide_lane // 8 == wide_row, 1.0, 0.0).astype(BF16)
        lane = lax.broadcasted_iota(jnp.int32, (320, 512), 1)
        row = lax.broadcasted_iota(jnp.int32, (320, 512), 0)
        same = (lane % 8) == (row % 8)
        for t in range(4):
            rows = jnp.concatenate([mix_rows[t + k, 8 * (4 - k):8 * (4 - k) + 8] for k in range(5)], axis=0)
            for ref, value in zip((mix_high, mix_low), split(rows)):
                wide = jnp.dot(value, widen, preferred_element_type=F32)
                wide = jnp.broadcast_to(wide[:, None, :], (40, 8, 512)).reshape(320, 512)
                ref[t] = jnp.where(same, wide, 0.0).astype(BF16)

    coupled[...] = jnp.zeros_like(coupled)
    for k in range(3):
        remote(mine, parts.at[k], part_send.at[k], part_recv.at[k], others[k]).wait_recv()
    mix_full[...] = mine[...] + parts[0] + parts[1] + parts[2]
    mix_rows[y + 2] = mix_full[...]
    for k in range(3):
        start(remote(mix_full, mix_rows.at[y + 2], row_send.at[k], row_recv.at[y + 2], mates[k]))
    for k in range(4):
        start(remote(mix_full, mix_rows.at[outer_spot], row_send.at[3 + k], row_recv.at[outer_spot], helpers[k]))
    own.wait()
    convert_x(0, 0, 4)

    for zl in range(2):
        wait_p(0, zl)
    for zl_right, zl_left in ((0, 1), (1, 0)):
        start(remote(raw.at[0, zl_right], raw.at[1, zl_right], p_send.at[0, zl_right],
                     p_recv.at[1, zl_right], to_right_x))
        start(remote(raw.at[0, zl_left], raw.at[2, zl_left], p_send.at[1, zl_left],
                     p_recv.at[2, zl_left], to_left_x))
    convert_p(0)
    unit_slot(0, 0)

    early, late = ((1, 0), (2, 1)), ((1, 1), (2, 0))
    for b, s in early:
        wait_x(b, 0, s)
        start(forward_x(0, s))
        to_sibling(b, 0, s)
    take_extra(early, True)
    for zl in range(2):
        wait_p(1 + zl, zl)
        forward_p(zl)

    for w in range(8):
        @pl.when(w != y + 2)
        def _():
            remote(mix_full, mix_rows.at[w], row_send.at[0], row_recv.at[w], mates[0]).wait_recv()

    build_mix()

    wait_p(1, 1)
    convert_p(1)
    wait_p(2, 0)
    convert_p(2)
    unit_first(0)
    mix(z_first, 0, 0, first_part)
    for b, s in late:
        wait_x(b, 0, s)
        to_sibling(b, 0, s)
    take_extra(late, False)
    pass_extra(early)
    pass_extra(late)
    for b in (1, 2):
        convert_x(b, 2 * core, 2)
        wait_sibling(b)
        convert_x(b, 2 * (1 - core), 2)
        unit_slot(0, b)
        unit_first(b)
        mix(z_first, 0, b, first_part)

    last = ((3, 0), (3, 1))
    for b, s in last:
        wait_x(b, 0, s)
        to_sibling(b, 0, s)
    take_extra(last, False)
    wait_p(3, 0)
    wait_p(3, 1)
    convert_p(3)
    unit_slot(3, 0)
    mix(z_second, 0, 0, second_part)
    pass_extra(last)
    convert_x(3, 2 * core, 2)
    wait_sibling(3)
    convert_x(3, 2 * (1 - core), 2)
    unit_first(3)
    mix(z_first, 0, 3, first_part)
    send_coupled(first_part)
    for b in (1, 2):
        unit_slot(3, b)
        mix(z_second, b * 8, b, second_part)
    unit_slot(0, 3)
    unit_slot(3, 3)
    mix(z_second, 24, 3, second_part)
    send_coupled(second_part)

    for part in (first_part, second_part):
        for k in range(4):
            pltpu.make_async_copy(coupled.at[0, 0], near.at[part, k], near_sem.at[part, k]).wait()
            pltpu.make_async_copy(coupled.at[0, 0], far.at[part, k], far_sem.at[part, k]).wait()
            at = part * 128 + k * 32
            cols = blocks[0, :, pl.ds(pl.multiple_of(mi * 256 + at, 32), 32), :]
            out[:, pl.ds(pl.multiple_of(at, 32), 32), :] = (
                shift[...] * cols + turn[...] * pltpu.roll(cols, 64, 2) - (near[part, k] + far[part, k])
            )

    for copy in sent:
        copy.wait_send()

    @pl.when(full)
    def _():
        for copy in sent_full:
            copy.wait_send()

    for part in range(2):
        for w in (0, 1, 6, 7):
            far_copy(part, w).wait_send()
        for w in (2, 3, 4, 5):
            @pl.when(y != w - 2)
            def _():
                near_copy(part, w).wait_send()


def filter_step(columns, panels, mine, shift, turn):
    dma = pltpu.SemaphoreType.DMA
    vmem = pl.BlockSpec(memory_space=pltpu.VMEM)
    anywhere = pl.BlockSpec(memory_space=pl.ANY)
    return pl.pallas_call(
        kernel,
        out_shape=jax.ShapeDtypeStruct((8, 256, 128), F32),
        in_specs=[anywhere, anywhere, vmem, vmem, vmem],
        out_specs=vmem,
        scratch_shapes=[
            pltpu.VMEM((4, 2, 2, 2, 32, NB), F32),
            pltpu.VMEM((16, 2, 32, NB), BF16),
            pltpu.VMEM((16, 2, 32, NB), BF16),
            pltpu.VMEM((4, 8, NB, 128), F32),
            pltpu.VMEM((16, NB, 256), BF16),
            pltpu.VMEM((16, NB, 256), BF16),
            pltpu.VMEM((8, 8, 32, 128), F32),
            pltpu.VMEM((32, 8, 32, 128), F32),
            pltpu.VMEM((3, 40, 128), F32),
            pltpu.VMEM((40, 128), F32),
            pltpu.VMEM((8, 40, 128), F32),
            pltpu.VMEM((4, 320, 512), BF16),
            pltpu.VMEM((4, 320, 512), BF16),
            pltpu.VMEM((2, 8, 8, 32, 128), F32),
            pltpu.VMEM((2, 4, 8, 32, 128), F32),
            pltpu.VMEM((2, 4, 8, 32, 128), F32),
            dma, dma((2,)), dma((3, 2)), dma((4, 2)),
            dma((2, 2, 2)), dma((2, 2)), dma((4, 2)), dma((4, 2, 2)), dma((4, 2, 2)), dma((4, 2, 2)),
            dma((3,)), dma((3,)), dma((7,)), dma((8,)), dma((2, 8)), dma((2, 4)), dma((2, 4)),
        ],
        compiler_params=pltpu.CompilerParams(
            collective_id=0, has_side_effects=True, vmem_limit_bytes=60 * 2**20
        ),
        cost_estimate=pl.CostEstimate(flops=30_000_000_000, bytes_accessed=40_000_000, transcendentals=0),
        name="filter_step",
    )(columns, panels, mine, shift, turn)


def own_mixing(coefficients, channel_cols, used_slots, lambda_low, lambda_high):
    mi = lax.axis_index("mult")
    ci = lax.axis_index("chan")
    lane = jnp.arange(128, dtype=jnp.int32)
    order = lane % 8
    slot_ids = jnp.arange(MAXNZ, dtype=jnp.int32)
    live_slot = slot_ids[None, :] < used_slots[:, None]
    keep = live_slot[:, :, None] & (order >= lambda_low[:, :, None]) & (order < lambda_high[:, :, None])
    keep &= (order // 2 == mi) & (lane < 64)
    value = jnp.where(order % 2 == 0, coefficients[:, :, :1], coefficients[:, :, 1:])
    weights = jnp.where(keep, value, 0.0)
    local = channel_cols - (ci - 2) * 8
    distance = jnp.arange(5, dtype=jnp.int32)
    hit = local[None, :, :, None] == distance[:, None, None, None] * 8 + lane // 8
    return jnp.sum(jnp.where(hit, weights[None], 0.0), axis=2).reshape(40, 128)


def body(
    columns, panels, coefficients, channel_cols, used_slots, lambda_low, lambda_high, energies, contour
):
    mine = own_mixing(coefficients, channel_cols, used_slots, lambda_low, lambda_high)
    shift = jnp.broadcast_to((contour[0] - energies)[:, None, None], (8, 1, 128))
    lane = jnp.arange(128, dtype=jnp.int32)
    turn = jnp.where(lane < 64, -contour[1], contour[1])[None, None, :]
    return filter_step(columns, panels, mine, shift, turn)


def solution(mesh):
    return jax.shard_map(
        body,
        mesh=mesh,
        in_specs=(
            P("chan", None, None),
            P("mult", None, "chan", None),
            P("chan", None, "mult"),
            P("chan", None),
            P("chan"),
            P("chan", None),
            P("chan", None),
            P("chan"),
            P(),
        ),
        out_specs=P("chan", "mult", None),
        check_vma=False,
    )
```

time: 1170 us -> 162 us (0.14)
  waiting for transfers between devices: 888 us -> 0 us
  Pallas kernels: 0 us -> 147 us
  matrix products: 137 us -> 0 us
  local copies, waits for them, and re-layouts: 81.9 us -> 5.03 us
  other arithmetic: 27.3 us -> 5.51 us
  starting transfers between devices: 16 us -> 0 us
  between operations: 14 us -> 0.68 us
    ppermute x4 -> x0, waiting for transfers between devices: 687 us -> none  [shifted(): return lax.ppermute(value, axis, pairs)]
    all_gather x1 -> x0, waiting for transfers between devices: 162 us -> none  [apply_panels(): panel_part = lax.all_gather(panels, 'chan', axis=2, tiled=True)]
    pallas_call x0 -> x1, Pallas kernels: none -> 147 us  [filter_step(): pl.pallas_call(kernel, out_shape=jax.ShapeDtypeStruct((8, 256, 128), F32)...]
    dot_general x4 -> x0, matrix products: 137 us -> none  [the longest x1 57.2 us: apply_panels(): jnp.einsum('lrb,cbk->clrk', real_panel, operand, precision=lax.Precision....]
    concatenate x3 -> x0, local copies, waits for them, and re-layouts: 52.4 us -> none  [the longest x2 51.3 us: body(): window = jnp.concatenate(nearby[:R] + [product] + nearby[R:], axis=0)]
    reduce_scatter x1 -> x0, waiting for transfers between devices: 39.1 us -> none  [body(): summed = lax.psum_scatter(-coupled, 'mult', scatter_dimension=1, tiled=True)]
    unnamed x28 -> x1, local copies, waits for them, and re-layouts: 26.8 us -> 2.27 us
    ppermute x4 -> x0, starting transfers between devices: 15.9 us -> none  [shifted(): return lax.ppermute(value, axis, pairs)]
  transfers between devices with their start and end apart: 6 -> 0, of which waited for: 5 -> 0; matrix products, arithmetic and copies ran while one was open for 3% -> 0% of each run, Pallas kernels for 0% -> 0%
where the time goes in v2:
time: 162 us; the launch traced here: 159 us
  Pallas kernels  147 us (91%)
  other arithmetic  5.51 us (3%)
  local copies, waits for them, and re-layouts  5.03 us (3%)
    pallas_call x1, Pallas kernels, filter_step(): pl.pallas_call(kernel, out_shape=jax.ShapeDtypeStruct((8, 256, 128), F32)...  147 us

profile of v2, /device:TPU:1, one launch (start us, length us, event | category | flops | bytes accessed | tf_op | source)
XLA Modules:
  0.0 158.7 jit_solution(3289147961978280981)
XLA Ops:
  0.0 0.7 iota_compare_fusion
  0.8 1.3 fusion.2
  2.7 1.2 compare_select_fusion.turn
  3.9 1.2 broadcast_subtract_fusion.1
  5.1 0.1 broadcast_add_fusion
  5.2 0.7 broadcast_in_dim.75.shift
  5.9 0.7 broadcast_subtract_fusion
  6.6 0.8 fusion.1
  7.3 0.9 select_select_fusion
  8.2 0.7 select_reduce_fusion
  8.9 147.4 %filter_step.1 = f32[8,256,128]{2,1,0:T(8,128)} custom-call(f32[8,1024,128]{2,1,0:T(8,128)} %columns.1, f32[2,2,32,1024]{3,2,1,0:T(8,128)} %panels.1, f32[40,128]{1,0:T(8,128)} %bitcast.9, f32[8,1,128]{2,1,0:T(1,128)} %broadcast_in_dim.75.shift, f32[1,1,128]{2,1,0:T(1,128)} %compare_select_fusion.turn), custom_call_target="tpu_custom_call" | custom-call | flops 30000001024 | bytes 40000000 | tf_op jit(solution)/shard_map/filter_step/pallas_call | solution.py:412
  156.4 2.3 %copy.17 = f32[8,256,128]{2,1,0:T(8,128)} copy(f32[8,256,128]{2,1,0:T(8,128)} %filter_step.1) | data formatting | bytes 2097152
  (4 shorter events, 0.0 us)

commit v3 on v2

--- a/solution.py
+++ b/solution.py
@@ -27,12 +27,39 @@
     return jnp.where(lane < 64, -rolled, rolled)
 
 
+def own_mixing(coefficients, channel_cols, lambda_low, lambda_high, used_slots, mine):
+    mi = lax.axis_index("mult")
+    ci = lax.axis_index("chan")
+    lane = lax.broadcasted_iota(jnp.int32, (8, 128), 1)
+    row = lax.broadcasted_iota(jnp.int32, (8, 128), 0)
+    order = lane % 8
+    used = jnp.zeros((8, 128), jnp.int32)
+    for i in range(8):
+        used = jnp.where(row == i, used_slots[i], used)
+    own_order = (order // 2 == mi) & (lane < 64)
+
+    def wide(ref_value, s):
+        return jnp.broadcast_to(ref_value[:, s:s + 1], (8, 128))
+
+    even, odd = coefficients[0], coefficients[1]
+    low, high, cols = lambda_low[...], lambda_high[...], channel_cols[...]
+    sums = [jnp.zeros((8, 128), F32) for _ in range(5)]
+    for s in range(MAXNZ):
+        value = jnp.where(order % 2 == 0, wide(even, s), wide(odd, s))
+        keep = own_order & (used > s) & (order >= wide(low, s)) & (order < wide(high, s))
+        value = jnp.where(keep, value, 0.0)
+        local = wide(cols, s) - (ci - 2) * 8 - lane // 8
+        for d in range(5):
+            sums[d] += jnp.where(local == d * 8, value, 0.0)
+    mine[...] = jnp.concatenate(sums, axis=0)
+
+
 def kernel(
-    columns, panels, mine, shift, turn, out,
+    columns, panels, coefficients, channel_cols, lambda_low, lambda_high, used_slots, energies, contour, out,
     raw, p_high, p_low, blocks, x_high, x_low, z_first, z_second,
-    parts, mix_full, mix_rows, mix_high, mix_low, coupled, near, far,
+    mine, parts, mix_rows, mix_high, mix_low, coupled, near, far,
     own_sem, first_send, p_send, p_recv, x_send, f_send, z_send, x_recv, s_send, s_recv,
-    part_send, part_recv, row_send, row_recv, c_send, near_sem, far_sem,
+    part_send, part_recv, row_send, row_recv, pair_send, pair_recv, near_send, near_sem, far_send, far_sem,
 ):
     mi = lax.axis_index("mult")
     ci = lax.axis_index("chan")
@@ -61,21 +88,20 @@
     first_part, second_part = x % 2, 1 - x % 2
 
     group = ci // 4
-    below, above = (group + 7) % 8, (group + 1) % 8
-    owners = [(mi, below * 4 + 2), (mi, below * 4 + 3)]
-    owners += [(mi, group * 4 + k) for k in range(4)]
-    owners += [(mi, above * 4), (mi, above * 4 + 1)]
-    outer = jnp.where(y < 2, below, above)
-    outer_spot = jnp.where(y < 2, y + 6, y - 2)
-    helpers = [(mi, outer * 4 + k) for k in range(4)]
+    below = (mi, (group + 7) % 8 * 4 + y)
+    above = (mi, (group + 1) % 8 * 4 + y)
     mates = [(mi, group * 4 + (y + k) % 4) for k in range(1, 4)]
     others = [((mi + k) % 4, ci) for k in range(1, 4)]
 
     barrier = pltpu.get_barrier_semaphore()
-    peers = [to_left_x, to_right_x] + targets + sources + others + mates + helpers
-    peers += [owners[w] for w in (0, 1, 6, 7)]
+    peers = [to_left_x, to_right_x, below, above] + targets + sources + others + mates
     for peer in peers:
         pl.semaphore_signal(barrier, inc=1, device_id=peer, device_id_type=MESH)
+
+    own = pltpu.make_async_copy(columns, blocks.at[0], own_sem)
+    own.start()
+    own_mixing(coefficients, channel_cols, lambda_low, lambda_high, used_slots, mine)
+    coupled[...] = jnp.zeros_like(coupled)
     pl.semaphore_wait(barrier, len(peers))
 
     def remote(src, dst, send_sem, recv_sem, peer):
@@ -108,15 +134,13 @@
         return copies
 
     common, extra = own_copies(0), own_copies(1)
-    for copy in common[:2]:
-        start(copy)
 
     @pl.when(full)
     def _():
         for copy in extra[:2]:
             copy.start()
 
-    for copy in common[2:]:
+    for copy in common[:2]:
         start(copy)
 
     @pl.when(full)
@@ -124,10 +148,9 @@
         for copy in extra[2:]:
             copy.start()
 
+    for copy in common[2:]:
+        start(copy)
     sent_full += extra
-
-    own = pltpu.make_async_copy(columns, blocks.at[0], own_sem)
-    own.start()
     for k in range(3):
         start(remote(mine, parts.at[2 - k], part_send.at[k], part_recv.at[2 - k], others[k]))
 
@@ -264,21 +287,45 @@
 
         lax.fori_loop(0, 2, step, 0)
 
-    def far_copy(part, w):
-        return remote(coupled.at[part, w], far.at[part, y], c_send.at[part, w], far_sem.at[part, y], owners[w])
-
-    def near_copy(part, w):
-        return remote(coupled.at[part, w], near.at[part, y], c_send.at[part, w], near_sem.at[part, y], owners[w])
-
-    def send_coupled(part):
-        for w in (0, 1, 6, 7):
-            far_copy(part, w).start()
-        for w in (2, 3, 4, 5):
-            @pl.when(y != w - 2)
-            def _():
-                near_copy(part, w).start()
-
-        pltpu.make_async_copy(coupled.at[part, y + 2], near.at[part, y], near_sem.at[part, y]).start()
+    def far_copies(part):
+        return [
+            remote(coupled.at[part, pl.ds(0, 2)], far.at[part, 1], far_send.at[part, 0], far_sem.at[part, 1], below),
+            remote(coupled.at[part, pl.ds(6, 2)], far.at[part, 0], far_send.at[part, 1], far_sem.at[part, 0], above),
+        ]
+
+    def near_copies(part):
+        return [
+            remote(coupled.at[part, 2 + (y + k) % 4], near.at[part, y], near_send.at[part, k - 1],
+                   near_sem.at[part, y], mates[k - 1])
+            for k in range(1, 4)
+        ]
+
+    def send_far(part):
+        for copy in far_copies(part):
+            start(copy)
+
+    def send_near(part):
+        for k in range(2):
+            ref = far.at[part, k]
+            remote(ref, ref, far_send.at[part, k], far_sem.at[part, k], below).wait_recv()
+            coupled[part, pl.ds(2 + 2 * k, 2)] += far[part, k]
+        for copy in near_copies(part):
+            start(copy)
+        near[part, y] = coupled[part, 2 + y]
+
+    def finish(part):
+        for k in range(1, 4):
+            ref = near.at[part, (y + k) % 4]
+            remote(ref, ref, near_send.at[part, 0], near_sem.at[part, (y + k) % 4], mates[0]).wait_recv()
+        lane = lax.broadcasted_iota(jnp.int32, (32, 128), 1)
+        turn = jnp.where(lane < 64, -contour[1], contour[1])
+        for k in range(4):
+            at = part * 128 + k * 32
+            for i in range(8):
+                cols = blocks[0, i, pl.ds(pl.multiple_of(mi * 256 + at, 32), 32), :]
+                out[i, pl.ds(pl.multiple_of(at, 32), 32), :] = (
+                    (contour[0] - energies[i]) * cols + turn * pltpu.roll(cols, 64, 1) - near[part, k, i]
+                )
 
     def build_mix():
         wide_row = lax.broadcasted_iota(jnp.int32, (128, 512), 0)
@@ -294,15 +341,11 @@
                 wide = jnp.broadcast_to(wide[:, None, :], (40, 8, 512)).reshape(320, 512)
                 ref[t] = jnp.where(same, wide, 0.0).astype(BF16)
 
-    coupled[...] = jnp.zeros_like(coupled)
     for k in range(3):
         remote(mine, parts.at[k], part_send.at[k], part_recv.at[k], others[k]).wait_recv()
-    mix_full[...] = mine[...] + parts[0] + parts[1] + parts[2]
-    mix_rows[y + 2] = mix_full[...]
+    mix_rows[y + 2] = mine[...] + parts[0] + parts[1] + parts[2]
     for k in range(3):
-        start(remote(mix_full, mix_rows.at[y + 2], row_send.at[k], row_recv.at[y + 2], mates[k]))
-    for k in range(4):
-        start(remote(mix_full, mix_rows.at[outer_spot], row_send.at[3 + k], row_recv.at[outer_spot], helpers[k]))
+        start(remote(mix_rows.at[y + 2], mix_rows.at[y + 2], row_send.at[k], row_recv.at[y], mates[k]))
     own.wait()
     convert_x(0, 0, 4)
 
@@ -313,80 +356,72 @@
                      p_recv.at[1, zl_right], to_right_x))
         start(remote(raw.at[0, zl_left], raw.at[2, zl_left], p_send.at[1, zl_left],
                      p_recv.at[2, zl_left], to_left_x))
+    for k in range(1, 4):
+        ref = mix_rows.at[2 + (y + k) % 4]
+        remote(ref, ref, row_send.at[0], row_recv.at[(y + k) % 4], mates[0]).wait_recv()
+    start(remote(mix_rows.at[pl.ds(2, 2)], mix_rows.at[pl.ds(6, 2)], pair_send.at[0], pair_recv.at[0], below))
+    start(remote(mix_rows.at[pl.ds(4, 2)], mix_rows.at[pl.ds(0, 2)], pair_send.at[1], pair_recv.at[1], above))
     convert_p(0)
     unit_slot(0, 0)
 
-    early, late = ((1, 0), (2, 1)), ((1, 1), (2, 0))
+    early, late, last = ((1, 0), (2, 1)), ((1, 1), (2, 0)), ((3, 0), (3, 1))
+    take_extra(early, True)
     for b, s in early:
         wait_x(b, 0, s)
         start(forward_x(0, s))
         to_sibling(b, 0, s)
-    take_extra(early, True)
+    for k in range(2):
+        ref = mix_rows.at[pl.ds(6 - 6 * k, 2)]
+        remote(ref, ref, pair_send.at[k], pair_recv.at[k], below).wait_recv()
     for zl in range(2):
         wait_p(1 + zl, zl)
         forward_p(zl)
-
-    for w in range(8):
-        @pl.when(w != y + 2)
-        def _():
-            remote(mix_full, mix_rows.at[w], row_send.at[0], row_recv.at[w], mates[0]).wait_recv()
-
     build_mix()
-
+    take_extra(late, False)
+    for b, s in late:
+        wait_x(b, 0, s)
+        to_sibling(b, 0, s)
     wait_p(1, 1)
     convert_p(1)
     wait_p(2, 0)
     convert_p(2)
     unit_first(0)
-    mix(z_first, 0, 0, first_part)
-    for b, s in late:
-        wait_x(b, 0, s)
-        to_sibling(b, 0, s)
-    take_extra(late, False)
     pass_extra(early)
     pass_extra(late)
+    mix(z_first, 0, 0, first_part)
     for b in (1, 2):
         convert_x(b, 2 * core, 2)
+    for b in (1, 2):
         wait_sibling(b)
         convert_x(b, 2 * (1 - core), 2)
         unit_slot(0, b)
-        unit_first(b)
-        mix(z_first, 0, b, first_part)
-
-    last = ((3, 0), (3, 1))
+    take_extra(last, False)
     for b, s in last:
         wait_x(b, 0, s)
         to_sibling(b, 0, s)
-    take_extra(last, False)
-    wait_p(3, 0)
-    wait_p(3, 1)
-    convert_p(3)
-    unit_slot(3, 0)
-    mix(z_second, 0, 0, second_part)
+    unit_first(1)
+    mix(z_first, 0, 1, first_part)
     pass_extra(last)
+    unit_first(2)
+    mix(z_first, 0, 2, first_part)
     convert_x(3, 2 * core, 2)
     wait_sibling(3)
     convert_x(3, 2 * (1 - core), 2)
     unit_first(3)
     mix(z_first, 0, 3, first_part)
-    send_coupled(first_part)
-    for b in (1, 2):
+    send_far(first_part)
+    wait_p(3, 0)
+    wait_p(3, 1)
+    convert_p(3)
+    unit_slot(0, 3)
+    for b in range(4):
         unit_slot(3, b)
         mix(z_second, b * 8, b, second_part)
-    unit_slot(0, 3)
-    unit_slot(3, 3)
-    mix(z_second, 24, 3, second_part)
-    send_coupled(second_part)
-
-    for part in (first_part, second_part):
-        for k in range(4):
-            pltpu.make_async_copy(coupled.at[0, 0], near.at[part, k], near_sem.at[part, k]).wait()
-            pltpu.make_async_copy(coupled.at[0, 0], far.at[part, k], far_sem.at[part, k]).wait()
-            at = part * 128 + k * 32
-            cols = blocks[0, :, pl.ds(pl.multiple_of(mi * 256 + at, 32), 32), :]
-            out[:, pl.ds(pl.multiple_of(at, 32), 32), :] = (
-                shift[...] * cols + turn[...] * pltpu.roll(cols, 64, 2) - (near[part, k] + far[part, k])
-            )
+    send_far(second_part)
+    send_near(second_part)
+    send_near(first_part)
+    finish(second_part)
+    finish(first_part)
 
     for copy in sent:
         copy.wait_send()
@@ -396,23 +431,16 @@
         for copy in sent_full:
             copy.wait_send()
 
-    for part in range(2):
-        for w in (0, 1, 6, 7):
-            far_copy(part, w).wait_send()
-        for w in (2, 3, 4, 5):
-            @pl.when(y != w - 2)
-            def _():
-                near_copy(part, w).wait_send()
-
-
-def filter_step(columns, panels, mine, shift, turn):
+
+def filter_step(*operands):
     dma = pltpu.SemaphoreType.DMA
     vmem = pl.BlockSpec(memory_space=pltpu.VMEM)
+    smem = pl.BlockSpec(memory_space=pltpu.SMEM)
     anywhere = pl.BlockSpec(memory_space=pl.ANY)
     return pl.pallas_call(
         kernel,
         out_shape=jax.ShapeDtypeStruct((8, 256, 128), F32),
-        in_specs=[anywhere, anywhere, vmem, vmem, vmem],
+        in_specs=[anywhere] * 2 + [vmem] * 4 + [smem] * 3,
         out_specs=vmem,
         scratch_shapes=[
             pltpu.VMEM((4, 2, 2, 2, 32, NB), F32),
@@ -423,51 +451,34 @@
             pltpu.VMEM((16, NB, 256), BF16),
             pltpu.VMEM((8, 8, 32, 128), F32),
             pltpu.VMEM((32, 8, 32, 128), F32),
+            pltpu.VMEM((40, 128), F32),
             pltpu.VMEM((3, 40, 128), F32),
-            pltpu.VMEM((40, 128), F32),
             pltpu.VMEM((8, 40, 128), F32),
             pltpu.VMEM((4, 320, 512), BF16),
             pltpu.VMEM((4, 320, 512), BF16),
             pltpu.VMEM((2, 8, 8, 32, 128), F32),
             pltpu.VMEM((2, 4, 8, 32, 128), F32),
-            pltpu.VMEM((2, 4, 8, 32, 128), F32),
+            pltpu.VMEM((2, 2, 2, 8, 32, 128), F32),
             dma, dma((2,)), dma((3, 2)), dma((4, 2)),
             dma((2, 2, 2)), dma((2, 2)), dma((4, 2)), dma((4, 2, 2)), dma((4, 2, 2)), dma((4, 2, 2)),
-            dma((3,)), dma((3,)), dma((7,)), dma((8,)), dma((2, 8)), dma((2, 4)), dma((2, 4)),
+            dma((3,)), dma((3,)), dma((3,)), dma((4,)), dma((2,)), dma((2,)),
+            dma((2, 3)), dma((2, 4)), dma((2, 2)), dma((2, 2)),
         ],
         compiler_params=pltpu.CompilerParams(
             collective_id=0, has_side_effects=True, vmem_limit_bytes=60 * 2**20
         ),
         cost_estimate=pl.CostEstimate(flops=30_000_000_000, bytes_accessed=40_000_000, transcendentals=0),
         name="filter_step",
-    )(columns, panels, mine, shift, turn)
-
-
-def own_mixing(coefficients, channel_cols, used_slots, lambda_low, lambda_high):
-    mi = lax.axis_index("mult")
-    ci = lax.axis_index("chan")
-    lane = jnp.arange(128, dtype=jnp.int32)
-    order = lane % 8
-    slot_ids = jnp.arange(MAXNZ, dtype=jnp.int32)
-    live_slot = slot_ids[None, :] < used_slots[:, None]
-    keep = live_slot[:, :, None] & (order >= lambda_low[:, :, None]) & (order < lambda_high[:, :, None])
-    keep &= (order // 2 == mi) & (lane < 64)
-    value = jnp.where(order % 2 == 0, coefficients[:, :, :1], coefficients[:, :, 1:])
-    weights = jnp.where(keep, value, 0.0)
-    local = channel_cols - (ci - 2) * 8
-    distance = jnp.arange(5, dtype=jnp.int32)
-    hit = local[None, :, :, None] == distance[:, None, None, None] * 8 + lane // 8
-    return jnp.sum(jnp.where(hit, weights[None], 0.0), axis=2).reshape(40, 128)
+    )(*operands)
 
 
 def body(
     columns, panels, coefficients, channel_cols, used_slots, lambda_low, lambda_high, energies, contour
 ):
-    mine = own_mixing(coefficients, channel_cols, used_slots, lambda_low, lambda_high)
-    shift = jnp.broadcast_to((contour[0] - energies)[:, None, None], (8, 1, 128))
-    lane = jnp.arange(128, dtype=jnp.int32)
-    turn = jnp.where(lane < 64, -contour[1], contour[1])[None, None, :]
-    return filter_step(columns, panels, mine, shift, turn)
+    return filter_step(
+        columns, panels, jnp.transpose(coefficients, (2, 0, 1)), channel_cols, lambda_low, lambda_high,
+        used_slots, energies, contour,
+    )
 
 
 def solution(mesh):

time: 162 us -> 147 us (0.907); the launches traced: 159 us -> 147 us
  other arithmetic: 5.51 us -> 0 us
  Pallas kernels: 147 us -> 143 us
    pallas_call x1, Pallas kernels: 147 us -> 143 us  [filter_step(): pl.pallas_call(kernel, out_shape=jax.ShapeDtypeStruct((8, 256, 128), F32)...]
    slice x2 -> x0, local copies, waits for them, and re-layouts: 2.09 us -> none  [the longest x1 1.31 us: body(): turn = jnp.where(lane < 64, -contour[1], contour[1])[None, None, :]]
    select_n x4 -> x0, other arithmetic: 2.05 us -> none  [the longest x1 1.19 us: body(): turn = jnp.where(lane < 64, -contour[1], contour[1])[None, None, :]]
    sub x2 -> x0, other arithmetic: 1.9 us -> none  [the longest x1 1.22 us: body(): contour[0] - energies]
    unnamed x1 -> x2, local copies, waits for them, and re-layouts: 2.27 us -> 3.57 us
where the time goes in v3:
time: 147 us
  Pallas kernels  143 us (97%)
  local copies, waits for them, and re-layouts  3.57 us (2%)
    pallas_call x1, Pallas kernels, filter_step(): pl.pallas_call(kernel, out_shape=jax.ShapeDtypeStruct((8, 256, 128), F32)...  143 us
    unnamed x2, local copies, waits for them, and re-layouts  3.57 us

profile of v3, /device:TPU:1, one launch (start us, length us, event | category | flops | bytes accessed | tf_op | source)
XLA Modules:
  0.0 146.7 jit_solution(333720020269625727)
XLA Ops:
  0.0 1.3 copy.12
  1.3 143.1 %filter_step.1 = f32[8,256,128]{2,1,0:T(8,128)} custom-call(f32[8,1024,128]{2,1,0:T(8,128)} %columns.1, f32[2,2,32,1024]{3,2,1,0:T(8,128)} %panels.1, f32[2,8,16]{2,1,0:T(8,128)} %bitcast.3, s32[8,16]{1,0:T(8,128)} %channel_cols.1, s32[8,16]{1,0:T(8,128)} %lambda_low.1, s32[8,16]{1,0:T(8,128)} %lambda_high.1, s32[8]{0:T(128)} %used_slots.1, f32[8]{0:T(128)} %energies.1, ...), custom_call_target="tpu_custom_call" | custom-call | flops 30000001024 | bytes 40000000 | tf_op jit(solution)/shard_map/filter_step/pallas_call | solution.py:440
  144.4 2.3 %copy.14 = f32[8,256,128]{2,1,0:T(8,128)} copy(f32[8,256,128]{2,1,0:T(8,128)} %filter_step.1) | data formatting | bytes 2097152

commit v4 on v3

--- a/solution.py
+++ b/solution.py
@@ -117,8 +117,17 @@
         copy.start()
         sent.append(copy)
 
+    for k in range(3):
+        start(remote(mine, parts.at[2 - k], part_send.at[k], part_recv.at[2 - k], others[k]))
+
     for k in range(2):
         start(remote(panels, raw.at[0, z_lo], first_send.at[k], p_recv.at[0, z_lo], targets[k]))
+
+    for k in range(3):
+        remote(mine, parts.at[k], part_send.at[k], part_recv.at[k], others[k]).wait_recv()
+    mix_rows[y + 2] = mine[...] + parts[0] + parts[1] + parts[2]
+    for k in range(3):
+        start(remote(mix_rows.at[y + 2], mix_rows.at[y + 2], row_send.at[k], row_recv.at[y], mates[k]))
 
     def channel(e, s):
         return 4 * core + 2 * e + s
@@ -151,8 +160,11 @@
     for copy in common[2:]:
         start(copy)
     sent_full += extra
-    for k in range(3):
-        start(remote(mine, parts.at[2 - k], part_send.at[k], part_recv.at[2 - k], others[k]))
+    for k in range(1, 4):
+        ref = mix_rows.at[2 + (y + k) % 4]
+        remote(ref, ref, row_send.at[0], row_recv.at[(y + k) % 4], mates[0]).wait_recv()
+    start(remote(mix_rows.at[pl.ds(2, 2)], mix_rows.at[pl.ds(6, 2)], pair_send.at[0], pair_recv.at[0], below))
+    start(remote(mix_rows.at[pl.ds(4, 2)], mix_rows.at[pl.ds(0, 2)], pair_send.at[1], pair_recv.at[1], above))
 
     def wait_p(slot, zl):
         ref = raw.at[slot, zl]
@@ -218,51 +230,64 @@
                     p_high[at, ri] = high
                     p_low[at, ri] = low
 
-    def convert_x(b, first, count):
+    def half(k):
+        return (core + k) % 2
+
+    def convert_x(b, k):
+        h = half(k)
+        for quarter in range(4):
+            high, low = split(blocks[b, 4 * h + quarter])
+            x_high[b, h, :, quarter * 128:quarter * 128 + 128] = high
+            x_low[b, h, :, quarter * 128:quarter * 128 + 128] = low
+
+    def multiply(ph, plo, b, h):
+        acc = jnp.dot(ph, x_high[b, h], preferred_element_type=F32)
+        acc += jnp.dot(plo, x_high[b, h], preferred_element_type=F32)
+        acc += jnp.dot(ph, x_low[b, h], preferred_element_type=F32)
+        return acc
+
+    def store(ref, acc, count, at, chan):
+        acc = acc.reshape(count, 2, 32, 512)
+        for quarter in range(4):
+            part = acc[..., quarter * 128:quarter * 128 + 128]
+            ref[chan + quarter, pl.ds(at, count)] = part[:, 0] + swap_halves(part[:, 1])
+
+    def each(run, halves):
         def step(k, carry):
-            piece = first + k
-            both = jnp.concatenate([blocks[b, 2 * piece], blocks[b, 2 * piece + 1]], axis=1)
-            high, low = split(both)
-            x_high[b * 4 + piece] = high
-            x_low[b * 4 + piece] = low
+            run(half(k))
             return carry
 
-        lax.fori_loop(0, count, step, 0)
-
-    def multiply(ph, plo, piece):
-        acc = jnp.dot(ph, x_high[piece], preferred_element_type=F32)
-        acc += jnp.dot(plo, x_high[piece], preferred_element_type=F32)
-        acc += jnp.dot(ph, x_low[piece], preferred_element_type=F32)
-        return acc
-
-    def store(ref, acc, count, at, chan):
-        acc = acc.reshape(count, 2, 32, 256)
-        for half in range(2):
-            part = acc[..., half * 128:half * 128 + 128]
-            ref[chan + half, pl.ds(at, count)] = part[:, 0] + swap_halves(part[:, 1])
-
-    def unit_slot(slot, b):
+        lax.fori_loop(halves[0], halves[-1] + 1, step, 0)
+
+    def unit_slot(slot, b, halves=(0, 1)):
         row_part, _, from_core = spots[slot]
         ats = [4 * zl + 2 * from_core for zl in range(2)]
 
-        def step(k, carry):
+        def run(h):
             ph = jnp.concatenate([p_high[pl.ds(row_part * 8 + at, 2)] for at in ats], axis=0)
             plo = jnp.concatenate([p_low[pl.ds(row_part * 8 + at, 2)] for at in ats], axis=0)
-            acc = multiply(ph.reshape(256, NB), plo.reshape(256, NB), b * 4 + k)
+            acc = multiply(ph.reshape(256, NB), plo.reshape(256, NB), b, h)
             for zl in range(2):
-                store(z_second, acc[zl * 128:zl * 128 + 128], 2, ats[zl], b * 8 + 2 * k)
-            return carry
-
-        lax.fori_loop(0, 4, step, 0)
-
-    def unit_first(b):
-        def step(k, carry):
-            ph = p_high[pl.ds(first_part * 8, 8)].reshape(512, NB)
-            plo = p_low[pl.ds(first_part * 8, 8)].reshape(512, NB)
-            store(z_first, multiply(ph, plo, b * 4 + k), 8, 0, 2 * k)
-            return carry
-
-        lax.fori_loop(0, 4, step, 0)
+                store(z_second, acc[zl * 128:zl * 128 + 128], 2, ats[zl], b * 8 + 4 * h)
+
+        each(run, halves)
+
+    def unit_part(part, ref, base, b, halves=(0, 1)):
+        def run(h):
+            ph = p_high[pl.ds(part * 8, 8)].reshape(512, NB)
+            plo = p_low[pl.ds(part * 8, 8)].reshape(512, NB)
+            store(ref, multiply(ph, plo, b, h), 8, 0, base + 4 * h)
+
+        each(run, halves)
+
+    def unit_first(b, halves=(0, 1)):
+        unit_part(first_part, z_first, 8 * (b == 2), b, halves)
+
+    def mix_first(b):
+        mix(z_first, 8 * (b == 2), b, first_part)
+
+    def mix_second(b):
+        mix(z_second, b * 8, b, second_part)
 
     at_y = [y, left_y, right_y, (y + 2) % 4]
 
@@ -341,13 +366,9 @@
                 wide = jnp.broadcast_to(wide[:, None, :], (40, 8, 512)).reshape(320, 512)
                 ref[t] = jnp.where(same, wide, 0.0).astype(BF16)
 
-    for k in range(3):
-        remote(mine, parts.at[k], part_send.at[k], part_recv.at[k], others[k]).wait_recv()
-    mix_rows[y + 2] = mine[...] + parts[0] + parts[1] + parts[2]
-    for k in range(3):
-        start(remote(mix_rows.at[y + 2], mix_rows.at[y + 2], row_send.at[k], row_recv.at[y], mates[k]))
     own.wait()
-    convert_x(0, 0, 4)
+    for k in range(2):
+        convert_x(0, k)
 
     for zl in range(2):
         wait_p(0, zl)
@@ -356,11 +377,6 @@
                      p_recv.at[1, zl_right], to_right_x))
         start(remote(raw.at[0, zl_left], raw.at[2, zl_left], p_send.at[1, zl_left],
                      p_recv.at[2, zl_left], to_left_x))
-    for k in range(1, 4):
-        ref = mix_rows.at[2 + (y + k) % 4]
-        remote(ref, ref, row_send.at[0], row_recv.at[(y + k) % 4], mates[0]).wait_recv()
-    start(remote(mix_rows.at[pl.ds(2, 2)], mix_rows.at[pl.ds(6, 2)], pair_send.at[0], pair_recv.at[0], below))
-    start(remote(mix_rows.at[pl.ds(4, 2)], mix_rows.at[pl.ds(0, 2)], pair_send.at[1], pair_recv.at[1], above))
     convert_p(0)
     unit_slot(0, 0)
 
@@ -370,12 +386,12 @@
         wait_x(b, 0, s)
         start(forward_x(0, s))
         to_sibling(b, 0, s)
+    for zl in range(2):
+        wait_p(1 + zl, zl)
+        forward_p(zl)
     for k in range(2):
         ref = mix_rows.at[pl.ds(6 - 6 * k, 2)]
         remote(ref, ref, pair_send.at[k], pair_recv.at[k], below).wait_recv()
-    for zl in range(2):
-        wait_p(1 + zl, zl)
-        forward_p(zl)
     build_mix()
     take_extra(late, False)
     for b, s in late:
@@ -388,35 +404,41 @@
     unit_first(0)
     pass_extra(early)
     pass_extra(late)
-    mix(z_first, 0, 0, first_part)
+    mix_first(0)
     for b in (1, 2):
-        convert_x(b, 2 * core, 2)
-    for b in (1, 2):
-        wait_sibling(b)
-        convert_x(b, 2 * (1 - core), 2)
-        unit_slot(0, b)
+        convert_x(b, 0)
+        unit_slot(0, b, (0,))
+    unit_first(1, (0,))
     take_extra(last, False)
     for b, s in last:
         wait_x(b, 0, s)
         to_sibling(b, 0, s)
-    unit_first(1)
-    mix(z_first, 0, 1, first_part)
+    unit_first(2, (0,))
+    wait_sibling(1)
+    convert_x(1, 1)
+    unit_slot(0, 1, (1,))
+    unit_first(1, (1,))
     pass_extra(last)
-    unit_first(2)
-    mix(z_first, 0, 2, first_part)
-    convert_x(3, 2 * core, 2)
+    mix_first(1)
+    wait_sibling(2)
+    convert_x(2, 1)
+    unit_slot(0, 2, (1,))
+    unit_first(2, (1,))
+    mix_first(2)
+    convert_x(3, 0)
     wait_sibling(3)
-    convert_x(3, 2 * (1 - core), 2)
+    convert_x(3, 1)
     unit_first(3)
-    mix(z_first, 0, 3, first_part)
+    mix_first(3)
     send_far(first_part)
     wait_p(3, 0)
     wait_p(3, 1)
     convert_p(3)
-    unit_slot(0, 3)
-    for b in range(4):
+    for b in range(3):
         unit_slot(3, b)
-        mix(z_second, b * 8, b, second_part)
+        mix_second(b)
+    unit_part(second_part, z_second, 24, 3)
+    mix_second(3)
     send_far(second_part)
     send_near(second_part)
     send_near(first_part)
@@ -447,9 +469,9 @@
             pltpu.VMEM((16, 2, 32, NB), BF16),
             pltpu.VMEM((16, 2, 32, NB), BF16),
             pltpu.VMEM((4, 8, NB, 128), F32),
-            pltpu.VMEM((16, NB, 256), BF16),
-            pltpu.VMEM((16, NB, 256), BF16),
-            pltpu.VMEM((8, 8, 32, 128), F32),
+            pltpu.VMEM((4, 2, NB, 512), BF16),
+            pltpu.VMEM((4, 2, NB, 512), BF16),
+            pltpu.VMEM((16, 8, 32, 128), F32),
             pltpu.VMEM((32, 8, 32, 128), F32),
             pltpu.VMEM((40, 128), F32),
             pltpu.VMEM((3, 40, 128), F32),

time: 147 us -> 129 us (0.88)
  Pallas kernels: 143 us -> 126 us
    pallas_call x1, Pallas kernels: 143 us -> 126 us  [filter_step(): pl.pallas_call(kernel, out_shape=jax.ShapeDtypeStruct((8, 256, 128), F32)...]
where the time goes in v4:
time: 129 us
  Pallas kernels  126 us (98%)
  local copies, waits for them, and re-layouts  3.57 us (3%)
    pallas_call x1, Pallas kernels, filter_step(): pl.pallas_call(kernel, out_shape=jax.ShapeDtypeStruct((8, 256, 128), F32)...  126 us
    unnamed x2, local copies, waits for them, and re-layouts  3.57 us

profile of v4, /device:TPU:1, one launch (start us, length us, event | category | flops | bytes accessed | tf_op | source)
XLA Modules:
  0.0 129.3 jit_solution(10935833056123450486)
XLA Ops:
  0.0 1.3 %copy.12 = f32[8,16,2]{1,0,2:T(8,128)} copy(f32[8,16,2]{1,2,0:T(2,128)} %param.11) | data formatting | bytes 2048 | tf_op args[2]
  1.3 125.7 %filter_step.1 = f32[8,256,128]{2,1,0:T(8,128)} custom-call(f32[8,1024,128]{2,1,0:T(8,128)} %columns.1, f32[2,2,32,1024]{3,2,1,0:T(8,128)} %panels.1, f32[2,8,16]{2,1,0:T(8,128)} %bitcast.3, s32[8,16]{1,0:T(8,128)} %channel_cols.1, s32[8,16]{1,0:T(8,128)} %lambda_low.1, s32[8,16]{1,0:T(8,128)} %lambda_high.1, s32[8]{0:T(128)} %used_slots.1, f32[8]{0:T(128)} %energies.1, ...), custom_call_target="tpu_custom_call" | custom-call | flops 30000001024 | bytes 40000000 | tf_op jit(solution)/shard_map/filter_step/pallas_call | solution.py:462
  127.0 2.3 %copy.14 = f32[8,256,128]{2,1,0:T(8,128)} copy(f32[8,256,128]{2,1,0:T(8,128)} %filter_step.1) | data formatting | bytes 2097152

commit v5 on v4

--- a/solution.py
+++ b/solution.py
@@ -408,11 +408,11 @@
     for b in (1, 2):
         convert_x(b, 0)
         unit_slot(0, b, (0,))
-    unit_first(1, (0,))
     take_extra(last, False)
     for b, s in last:
         wait_x(b, 0, s)
         to_sibling(b, 0, s)
+    unit_first(1, (0,))
     unit_first(2, (0,))
     wait_sibling(1)
     convert_x(1, 1)

time: 129 us -> 128 us (level)
  Pallas kernels: 126 us -> 124 us
    pallas_call x1, Pallas kernels: 126 us -> 124 us  [filter_step(): pl.pallas_call(kernel, out_shape=jax.ShapeDtypeStruct((8, 256, 128), F32)...]
where the time goes in v5:
time: 128 us
  Pallas kernels  124 us (97%)
  local copies, waits for them, and re-layouts  3.57 us (3%)
    pallas_call x1, Pallas kernels, filter_step(): pl.pallas_call(kernel, out_shape=jax.ShapeDtypeStruct((8, 256, 128), F32)...  124 us
    unnamed x2, local copies, waits for them, and re-layouts  3.57 us

profile of v5, /device:TPU:1, one launch (start us, length us, event | category | flops | bytes accessed | tf_op | source)
XLA Modules:
  0.0 127.6 jit_solution(1159972278965984181)
XLA Ops:
  0.0 1.3 %copy.12 = f32[8,16,2]{1,0,2:T(8,128)} copy(f32[8,16,2]{1,2,0:T(2,128)} %param.11) | data formatting | bytes 2048 | tf_op args[2]
  1.3 124.1 %filter_step.1 = f32[8,256,128]{2,1,0:T(8,128)} custom-call(f32[8,1024,128]{2,1,0:T(8,128)} %columns.1, f32[2,2,32,1024]{3,2,1,0:T(8,128)} %panels.1, f32[2,8,16]{2,1,0:T(8,128)} %bitcast.3, s32[8,16]{1,0:T(8,128)} %channel_cols.1, s32[8,16]{1,0:T(8,128)} %lambda_low.1, s32[8,16]{1,0:T(8,128)} %lambda_high.1, s32[8]{0:T(128)} %used_slots.1, f32[8]{0:T(128)} %energies.1, ...), custom_call_target="tpu_custom_call" | custom-call | flops 30000001024 | bytes 40000000 | tf_op jit(solution)/shard_map/filter_step/pallas_call | solution.py:462
  125.4 2.3 %copy.14 = f32[8,256,128]{2,1,0:T(8,128)} copy(f32[8,256,128]{2,1,0:T(8,128)} %filter_step.1) | data formatting | bytes 2097152
